TPU v7x, 256 devices: a whole 4x4x8 slice. The times are simulated.
256 devices in a mesh: wide: 32 (over x_hi, z, core), narrow: 8 (over x_lo, y).
Axes of the slice: x: 4 (x_hi: 2, x_lo: 2; x = x_hi * 2 + x_lo), y: 4, z: 8, core: 2. Of those that a mesh axis runs over, the one named last changes fastest.
Arguments:
- field: bfloat16 [20, 256, 256, 256], P(None, 'wide', 'narrow'), may hold values from -6 to 6
- cotangent: bfloat16 [20, 256, 256, 256], P(None, 'wide', 'narrow'), may hold values from -6 to 6
- spectral_weight: float32 [2, 20, 20, 32, 32, 32], P(None, None, None, 'narrow', None, 'wide'), may hold values from -18 to 18
- local_weight: bfloat16 [20, 20], replicated, may hold values from -1.25 to 1.25
- local_bias: float32 [20], replicated, may hold values from -3 to 3
Outputs:
- activated: bfloat16 [20, 256, 256, 256], P(None, 'wide', 'narrow')
- field_grad: bfloat16 [20, 256, 256, 256], P(None, 'wide', 'narrow')
- weight_grad: float32 [2, 20, 20, 32, 32, 32], P(None, None, None, 'narrow', None, 'wide')
All inputs are finite; a program needn't handle non-finite values.
Results may differ from a plain program's by a relative error of at most 0.022.
Values may be sent and summed in bfloat16 or wider, within the bound.
No kernel may reach another device: no remote copies, remote signals or barrier semaphores. Data moves between devices by JAX's collectives and lax.ppermute only.
A program may use at most 128 MiB of HBM per device.

v0:
```python
import math

import jax
import jax.numpy as jnp
import ml_dtypes
import numpy as np
from jax import lax
from jax.experimental import pallas as pl
from jax.experimental.pallas import tpu as pltpu
from jax.sharding import PartitionSpec as P

N = 256
M = 32
C = 20
CP = 24
BF = jnp.bfloat16
F32 = jnp.float32
MIB = 1024 * 1024


def depth_tables():
    index = np.arange(N)
    freq = np.arange(M)
    angle = (2.0 * math.pi / N) * ((freq[:, None] * index[None, :]) % N)
    scale = 1.0 / math.sqrt(N)
    weights = np.where(freq == 0, 1.0, 2.0)[:, None]
    forward = (np.concatenate([np.cos(angle), -np.sin(angle)]) * scale).T
    inverse = np.concatenate([weights * np.cos(angle), -weights * np.sin(angle)]) * scale
    return forward, inverse


def lateral_angles():
    index = np.arange(N)
    base = np.arange(M)
    freq = np.where(base < M // 2, base, N - M + base)
    angle = (2.0 * math.pi / N) * ((freq[:, None] * index[None, :]) % N)
    scale = 1.0 / math.sqrt(N)
    return np.cos(angle) * scale, np.sin(angle) * scale


def bf16(array):
    return np.asarray(array, np.float32).astype(ml_dtypes.bfloat16)


def analysis_depth(table):
    out = np.zeros((2, N, 2, 2, 2, M))
    for half in range(2):
        real, imag = table[:, :M], table[:, M:]
        out[half, :, 0, 0, half] = real
        out[half, :, 0, 1, half] = imag
        out[half, :, 1, 0, half] = imag
        out[half, :, 1, 1, half] = -real
    return bf16(out.reshape(2, N, 256))


def synthesis_depth(table):
    out = np.zeros((2, 2, M, 2, N))
    for half in range(2):
        out[:, half, :, half] = table.reshape(2, M, N)
    return bf16(out.reshape(128, 512))


def second_tables():
    cosine, sine = lateral_angles()
    out = np.zeros((8, 8, 4, 4, 2, 4, M))
    for block in range(8):
        rows = slice(block * M, (block + 1) * M)
        for x in range(4):
            out[block, :, :, x, 0, x] = cosine[:, rows].reshape(8, 4, M)
            out[block, :, :, x, 1, x] = sine[:, rows].reshape(8, 4, M)
    out = out.reshape(8, 128, 256)
    return bf16(out), bf16(out.transpose(0, 2, 1))


def first_tables():
    cosine, sine = lateral_angles()
    cos_x = cosine.T.reshape(M, 8, M)
    sin_x = sine.T.reshape(M, 8, M)
    forward = np.zeros((M, 2, 8, 2, 4, M))
    inverse = np.zeros((M, 2, 8, 2, 4, M))
    for j in range(4):
        forward[:, 0, :, 0, j] = cos_x
        forward[:, 0, :, 1, j] = -sin_x
        forward[:, 1, :, 0, j] = sin_x
        forward[:, 1, :, 1, j] = cos_x
        inverse[:, 0, :, 0, j] = cos_x
        inverse[:, 0, :, 1, j] = -sin_x
        inverse[:, 1, :, 0, j] = sin_x
        inverse[:, 1, :, 1, j] = cos_x
    return bf16(forward.reshape(512, 256)), bf16(inverse.reshape(512, 256))


def permutation(rows, lanes, sizes):
    total = int(np.prod([sizes[d] for d in rows]))
    position = np.arange(total).reshape([sizes[d] for d in rows])
    order = position.transpose([rows.index(d) for d in lanes]).reshape(-1)
    out = np.zeros((total, total))
    out[order, np.arange(total)] = 1.0
    return bf16(out)


def dot(a, b):
    return jnp.dot(a, b, preferred_element_type=F32)


def dot_nt(a, b):
    return lax.dot_general(a, b, (((1,), (1,)), ((), ())), preferred_element_type=F32)


def dot_tn(a, b):
    return lax.dot_general(a, b, (((0,), (0,)), ((), ())), preferred_element_type=F32)


def params(limit=40):
    return pltpu.CompilerParams(vmem_limit_bytes=limit * MIB)


def cost(flops, bytes_accessed, transcendentals=0):
    return pl.CostEstimate(
        flops=flops, bytes_accessed=bytes_accessed, transcendentals=transcendentals
    )


def second_forward(planes_ref, table, out_ref, first, count):
    for c in range(0, count, 2):
        one = planes_ref[first + c]
        two = planes_ref[first + c + 1]
        stacked = jnp.concatenate(
            [
                jnp.concatenate([one[:, :128], two[:, :128]], axis=1),
                jnp.concatenate([one[:, 128:], two[:, 128:]], axis=1),
            ],
            axis=0,
        )
        got = dot(table, stacked).astype(BF)
        for q in range(2):
            out_ref[:, (c + q) * 16 : (c + q + 1) * 16, :] = got[
                :, q * 128 : (q + 1) * 128
            ].reshape(8, 16, 128)


def analyse_kernel(field_ref, depth_ref, table_ref, out_ref, planes_ref):
    count = field_ref.shape[0]
    low = field_ref[:, 0].reshape(count * 128, N)
    high = field_ref[:, 1].reshape(count * 128, N)
    planes = dot(low, depth_ref[0]) + dot(high, depth_ref[1])
    planes_ref[...] = planes.astype(BF).reshape(count, 128, N)
    second_forward(planes_ref, table_ref[...], out_ref, 0, count)


def analyse(field, depth, table):
    step = 4
    return pl.pallas_call(
        analyse_kernel,
        grid=(C // step,),
        in_specs=[
            pl.BlockSpec((step, 2, 4, M, N), lambda t: (t, 0, 0, 0, 0)),
            pl.BlockSpec((2, N, 256), lambda t: (0, 0, 0)),
            pl.BlockSpec((128, 256), lambda t: (0, 0)),
        ],
        out_specs=pl.BlockSpec((8, step * 16, 128), lambda t: (0, t, 0)),
        out_shape=jax.ShapeDtypeStruct((8, C * 16, 128), BF),
        scratch_shapes=[pltpu.VMEM((step, 128, 256), BF)],
        compiler_params=params(),
        cost_estimate=cost(2 * 20 * 256 * 256 * 256, 3 * MIB),
        name="analyse",
    )(field, depth, table)


def gather_kernel(in_ref, perm_ref, out_ref, sum_ref, rows_ref, turned_ref):
    total = in_ref[0].astype(F32)
    for source in range(1, 8):
        total = total + in_ref[source].astype(F32)
    sum_ref[0 : C * 16] = total
    sum_ref[C * 16 :] = jnp.zeros((64, 128), F32)
    rows_ref[...] = jnp.zeros((512, 128), F32)
    for x in range(4):
        for j in range(4):
            rows_ref[x * 128 + j * 32 : x * 128 + j * 32 + CP, :] = sum_ref[
                pl.ds(j * 4 + x, CP, stride=16), :
            ]
    got = dot_nt(perm_ref[...], rows_ref[...].astype(BF))
    for x in range(4):
        turned_ref[pl.ds(x, 128, stride=4), :] = got[:, x * 128 : (x + 1) * 128]
    out_ref[...] = turned_ref[...].astype(BF).reshape(32, 16, 128)


def gather(parts, perm):
    return pl.pallas_call(
        gather_kernel,
        out_shape=jax.ShapeDtypeStruct((32, 16, 128), BF),
        scratch_shapes=[
            pltpu.VMEM((C * 16 + 64, 128), F32),
            pltpu.VMEM((512, 128), F32),
            pltpu.VMEM((512, 128), F32),
        ],
        compiler_params=params(),
        cost_estimate=cost(2 * 128 * 128 * 512, MIB),
        name="gather",
    )(parts, perm)


def scatter_kernel(in_ref, perm_ref, out_ref, turned_ref, rows_ref):
    turned_ref[...] = in_ref[...].reshape(512, 128).astype(F32)
    for x in range(4):
        block = turned_ref[pl.ds(x, 128, stride=4), :].astype(BF)
        got = dot_tn(block, perm_ref[...])
        for j in range(4):
            rows_ref[pl.ds(j * 4 + x, CP, stride=16), :] = got[j * 32 : j * 32 + CP]
    value = rows_ref[0 : C * 16].astype(BF)
    for target in range(8):
        out_ref[target] = value


def scatter(lines, perm):
    return pl.pallas_call(
        scatter_kernel,
        out_shape=jax.ShapeDtypeStruct((8, C * 16, 128), BF),
        scratch_shapes=[
            pltpu.VMEM((512, 128), F32),
            pltpu.VMEM((CP * 16, 128), F32),
        ],
        compiler_params=params(),
        cost_estimate=cost(2 * 128 * 128 * 512, MIB),
        name="scatter",
    )(lines, perm)


def lane_group(shape):
    return lax.broadcasted_iota(jnp.int32, shape, 1) // M % 4


def to_modes(lines_ref, first_ref):
    got = dot_tn(lines_ref[...].reshape(512, 128), first_ref[...])
    group = lane_group((M, 256))
    out = jnp.zeros((M, 256), F32)
    for j in range(4):
        out = jnp.where(group == j, got[j * M : (j + 1) * M], out)
    return out[:, :128], out[:, 128:]


def from_modes(real, imag, inverse_ref, out_ref):
    both = jnp.concatenate([real, imag], axis=1)
    group = lane_group((M, 256))
    rows = [jnp.where(group == j, both, 0.0) for j in range(4)]
    stacked = jnp.concatenate(rows, axis=0).astype(BF)
    out_ref[...] = dot_nt(inverse_ref[...], stacked).astype(BF).reshape(32, 16, 128)


def mix_kernel(lines_ref, weight_ref, first_ref, inverse_ref, out_ref, spectrum_ref):
    real, imag = to_modes(lines_ref, first_ref)
    spectrum_ref[0] = real
    spectrum_ref[1] = imag
    mixed_real = jnp.zeros((CP, 128), F32)
    mixed_imag = jnp.zeros((CP, 128), F32)
    for c in range(C):
        w0 = weight_ref[c * CP : (c + 1) * CP, :]
        w1 = weight_ref[(C + c) * CP : (C + c + 1) * CP, :]
        s0 = real[c : c + 1]
        s1 = imag[c : c + 1]
        mixed_real = mixed_real + s0 * w0 - s1 * w1
        mixed_imag = mixed_imag + s0 * w1 + s1 * w0
    pad = jnp.zeros((M - CP, 128), F32)
    from_modes(
        jnp.concatenate([mixed_real, pad]),
        jnp.concatenate([mixed_imag, pad]),
        inverse_ref,
        out_ref,
    )


def mix_back_kernel(
    lines_ref, weight_ref, first_ref, inverse_ref, spectrum_ref, perm_ref, out_ref, pair_ref, acc_ref
):
    real, imag = to_modes(lines_ref, first_ref)
    both = jnp.concatenate([spectrum_ref[0], spectrum_ref[1], real, imag], axis=0)
    pair_ref[...] = dot_nt(perm_ref[...], both.astype(BF)).astype(BF).reshape(8, 16, 128)
    r0 = real[:CP]
    r1 = imag[:CP]
    acc_ref[...] = jnp.zeros((2, M, 128), F32)
    for c in range(C):
        w0 = weight_ref[c * CP : (c + 1) * CP, :]
        w1 = weight_ref[(C + c) * CP : (C + c + 1) * CP, :]
        acc_ref[0, c : c + 1, :] = jnp.sum(r0 * w0 + r1 * w1, axis=0, keepdims=True)
        acc_ref[1, c : c + 1, :] = jnp.sum(r1 * w0 - r0 * w1, axis=0, keepdims=True)
    from_modes(acc_ref[0], acc_ref[1], inverse_ref, out_ref)


def mix(lines, weight, first, inverse):
    return pl.pallas_call(
        mix_kernel,
        out_shape=[
            jax.ShapeDtypeStruct((32, 16, 128), BF),
            jax.ShapeDtypeStruct((2, M, 128), F32),
        ],
        compiler_params=params(),
        cost_estimate=cost(4 * 512 * 128 * 256, 2 * MIB),
        name="mix",
    )(lines, weight, first, inverse)


def mix_back(lines, weight, first, inverse, spectrum, perm):
    return pl.pallas_call(
        mix_back_kernel,
        out_shape=[
            jax.ShapeDtypeStruct((32, 16, 128), BF),
            jax.ShapeDtypeStruct((8, 16, 128), BF),
        ],
        scratch_shapes=[pltpu.VMEM((2, M, 128), F32)],
        compiler_params=params(),
        cost_estimate=cost(4 * 512 * 128 * 256, 2 * MIB),
        name="mix_back",
    )(lines, weight, first, inverse, spectrum, perm)


def weight_out_kernel(weight_ref, perm_ref, out_ref, rows_ref):
    for q in range(2 * C):
        rows_ref[q * CP : q * CP + C, :] = weight_ref[q]
        rows_ref[q * CP + C : (q + 1) * CP, :] = jnp.zeros((CP - C, 128), F32)
    got = dot_nt(perm_ref[...], rows_ref[...].astype(BF))
    out_ref[...] = got.astype(BF).reshape(8, 16, 2 * C * CP)


def weight_out(weight, perm):
    return pl.pallas_call(
        weight_out_kernel,
        out_shape=jax.ShapeDtypeStruct((8, 16, 2 * C * CP), BF),
        scratch_shapes=[pltpu.VMEM((2 * C * CP, 128), F32)],
        compiler_params=params(),
        cost_estimate=cost(2 * 128 * 128 * 960, MIB),
        name="weight_out",
    )(weight, perm)


def weight_in_kernel(in_ref, perm_ref, out_ref):
    out_ref[...] = dot_tn(in_ref[...].reshape(128, 2 * C * CP), perm_ref[...])


def weight_in(parts, perm):
    return pl.pallas_call(
        weight_in_kernel,
        out_shape=jax.ShapeDtypeStruct((2 * C * CP, 128), F32),
        compiler_params=params(),
        cost_estimate=cost(2 * 128 * 128 * 960, MIB),
        name="weight_in",
    )(parts, perm)


def outer_kernel(pair_ref, perm_ref, out_ref):
    modes = dot_tn(pair_ref[...].reshape(128, 128), perm_ref[...])
    s0, s1 = modes[0:M], modes[M : 2 * M]
    r0, r1 = modes[2 * M : 2 * M + C], modes[3 * M : 3 * M + C]
    for c in range(C):
        a, b = s0[c : c + 1], s1[c : c + 1]
        out_ref[0, c] = a * r0 + b * r1
        out_ref[1, c] = a * r1 - b * r0


def outer(pair, perm):
    return pl.pallas_call(
        outer_kernel,
        out_shape=jax.ShapeDtypeStruct((2, C, C, 128), F32),
        compiler_params=params(),
        cost_estimate=cost(2 * 128 * 128 * 128, MIB),
        name="outer",
    )(pair, perm)


def second_inverse(in_ref, table_ref, planes_ref):
    table = table_ref[...]
    lane = lax.broadcasted_iota(jnp.int32, (128, 256), 1) % 128
    for c in range(0, C, 2):
        both = jnp.concatenate(
            [in_ref[:, (c + q) * 16 : (c + q + 1) * 16, :].reshape(128, 128) for q in range(2)],
            axis=1,
        )
        got = dot(table, both)
        for q in range(2):
            cos_part = got[:128, q * 128 : (q + 1) * 128]
            sin_part = got[128:, q * 128 : (q + 1) * 128]
            turned = pltpu.roll(sin_part, 64, 1)
            value = jnp.where(lane[:, :128] < 64, cos_part - turned, cos_part + turned)
            planes_ref[c + q] = value.astype(BF)


def local_kernel(
    parts_ref,
    field_ref,
    cotangent_ref,
    inverse_ref,
    synth_ref,
    depth_ref,
    table_ref,
    local_ref,
    bias_ref,
    activated_ref,
    slope_ref,
    out_ref,
    planes_ref,
    turned_ref,
):
    step = pl.program_id(0)

    @pl.when(step == 0)
    def _():
        second_inverse(parts_ref, inverse_ref, planes_ref)

    rows = pl.ds(pl.multiple_of(step * 16, 16), 16)
    planes = planes_ref[:, rows, :].reshape(C * 16, 128)
    spatial = dot(planes, synth_ref[...])
    response = jnp.zeros((C * 16, 256), F32)
    for x in range(2):
        field = field_ref[:, x].reshape(C * 16, N)
        value = spatial[:, x * N : (x + 1) * N] + dot(local_ref[...], field) + bias_ref[...]
        square = value * value
        inner = value * (0.7978845608028654 + 0.7978845608028654 * 0.044715 * square)
        tanh = jnp.tanh(inner)
        half = 0.5 + 0.5 * tanh
        activated = value * half
        d_inner = 0.7978845608028654 + 3.0 * 0.7978845608028654 * 0.044715 * square
        d_gelu = half + (0.5 * value) * (1.0 - tanh * tanh) * d_inner
        cotangent = cotangent_ref[:, x].reshape(C * 16, N).astype(F32)
        slope = (cotangent * d_gelu).astype(BF)
        activated_ref[:, x] = activated.astype(BF).reshape(C, 16, N)
        slope_ref[:, x] = slope.reshape(C, 16, N)
        response = response + dot(slope, depth_ref[x])
    turned_ref[:, rows, :] = response.astype(BF).reshape(C, 16, 256)

    @pl.when(step == pl.num_programs(0) - 1)
    def _():
        second_forward(turned_ref, table_ref[...], out_ref, 0, C)


def whole(shape):
    return pl.BlockSpec(shape, lambda t: (0,) * len(shape))


GRID_BLOCK = (C, 2, None, 16, N)


def grid_spec():
    return pl.BlockSpec(GRID_BLOCK, lambda t: (0, 0, t // 2, t % 2, 0))


def local(parts, field, cotangent, inverse, synth, depth, table, weight, bias):
    grid_shape = jax.ShapeDtypeStruct((C, 2, 4, M, N), BF)
    return pl.pallas_call(
        local_kernel,
        grid=(8,),
        in_specs=[
            whole((8, C * 16, 128)),
            grid_spec(),
            grid_spec(),
            whole((256, 128)),
            whole((128, 512)),
            whole((2, N, 256)),
            whole((128, 256)),
            whole((C * 16, C * 16)),
            whole((C * 16, N)),
        ],
        out_specs=[grid_spec(), grid_spec(), whole((8, C * 16, 128))],
        out_shape=[grid_shape, grid_shape, jax.ShapeDtypeStruct((8, C * 16, 128), BF)],
        scratch_shapes=[pltpu.VMEM((C, 128, 128), BF), pltpu.VMEM((C, 128, 256), BF)],
        compiler_params=params(),
        cost_estimate=cost(3 * 10**9, 12 * MIB, 1310720),
        name="local",
    )(parts, field, cotangent, inverse, synth, depth, table, weight, bias)


def local_back_kernel(
    parts_ref, slope_ref, inverse_ref, synth_ref, local_ref, out_ref, planes_ref
):
    step = pl.program_id(0)

    @pl.when(step == 0)
    def _():
        second_inverse(parts_ref, inverse_ref, planes_ref)

    rows = pl.ds(pl.multiple_of(step * 16, 16), 16)
    planes = planes_ref[:, rows, :].reshape(C * 16, 128)
    spatial = dot(planes, synth_ref[...])
    for x in range(2):
        slope = slope_ref[:, x].reshape(C * 16, N)
        value = spatial[:, x * N : (x + 1) * N] + dot(local_ref[...], slope)
        out_ref[:, x] = value.astype(BF).reshape(C, 16, N)


def local_back(parts, slope, inverse, synth, weight):
    return pl.pallas_call(
        local_back_kernel,
        grid=(8,),
        in_specs=[
            whole((8, C * 16, 128)),
            grid_spec(),
            whole((256, 128)),
            whole((128, 512)),
            whole((C * 16, C * 16)),
        ],
        out_specs=grid_spec(),
        out_shape=jax.ShapeDtypeStruct((C, 2, 4, M, N), BF),
        scratch_shapes=[pltpu.VMEM((C, 128, 128), BF)],
        compiler_params=params(),
        cost_estimate=cost(2 * 10**9, 6 * MIB),
        name="local_back",
    )(parts, slope, inverse, synth, weight)


def exchange(value, axis):
    return lax.all_to_all(value, axis, split_axis=0, concat_axis=0, tiled=True)


def shards(field, cotangent, spectral_weight, local_weight, local_bias):
    forward, inverse = depth_tables()
    forward_b, inverse_b = analysis_depth(forward), analysis_depth(inverse.T)
    synth_f, synth_b = synthesis_depth(inverse), synthesis_depth(forward.T)
    second, second_back = second_tables()
    first, first_back = first_tables()
    block = lax.axis_index("narrow")
    table = lax.dynamic_index_in_dim(jnp.asarray(second), block, 0, keepdims=False)
    table_back = lax.dynamic_index_in_dim(jnp.asarray(second_back), block, 0, keepdims=False)

    sizes = {"s": 2, "p": 2, "k": 32, "J": 8, "j": 4, "i": 4}
    perm_line = permutation("ksp", "spk", sizes)
    perm_weight = permutation("Jji", "iJj", sizes)
    perm_modes = permutation("Jji", "jJi", sizes)
    spread = np.zeros((C * 16, C))
    spread[np.arange(C * 16), np.arange(C * 16) // 16] = 1.0
    same = np.equal(np.arange(C * 16)[:, None] % 16, np.arange(C * 16)[None, :] % 16)
    spread, same = jnp.asarray(bf16(spread)), jnp.asarray(bf16(same))
    wide_weight = jnp.dot(jnp.dot(spread, local_weight), spread.T) * same
    wide_weight_back = wide_weight.T
    bias = jnp.broadcast_to(jnp.repeat(local_bias, 16)[:, None], (C * 16, N))

    shape = field.shape
    grid_field = field.reshape(C, 2, 4, M, N)
    grid_cotangent = cotangent.reshape(C, 2, 4, M, N)

    weight = weight_in(
        exchange(weight_out(spectral_weight.reshape(2 * C, C, 128), perm_weight), "narrow"),
        perm_modes,
    )
    parts = exchange(analyse(grid_field, forward_b, table), "narrow")
    lines = exchange(gather(parts, perm_line), "wide")
    lines, spectrum = mix(lines, weight, first, first_back)
    lines = exchange(lines, "wide")
    parts = exchange(scatter(lines, perm_line), "narrow")
    activated, slope, parts = local(
        parts,
        grid_field,
        grid_cotangent,
        table_back,
        synth_f,
        inverse_b,
        table,
        wide_weight,
        bias,
    )
    parts = exchange(parts, "narrow")
    lines = exchange(gather(parts, perm_line), "wide")
    lines, pair = mix_back(lines, weight, first, first_back, spectrum, perm_modes)
    lines = exchange(lines, "wide")
    weight_grad = outer(exchange(pair, "narrow"), perm_weight)
    parts = exchange(scatter(lines, perm_line), "narrow")
    field_grad = local_back(parts, slope, table_back, synth_b, wide_weight_back)
    return (
        activated.reshape(shape),
        field_grad.reshape(shape),
        weight_grad.reshape(spectral_weight.shape),
    )


def solution(mesh):
    return jax.shard_map(
        shards,
        mesh=mesh,
        in_specs=(
            P(None, "wide", "narrow", None),
            P(None, "wide", "narrow", None),
            P(None, None, None, "narrow", None, "wide"),
            P(),
            P(),
        ),
        out_specs=(
            P(None, "wide", "narrow", None),
            P(None, "wide", "narrow", None),
            P(None, None, None, "narrow", None, "wide"),
        ),
        check_vma=False,
    )
```

profile of v0, /device:TPU:2, one launch (start us, length us, event | category | flops | bytes accessed | tf_op | source)
XLA Modules:
  0.0 181.0 jit_solution(9905425232152817014)
XLA Ops:
  0.6 0.9 dynamic-slice_bitcast_fusion.1.table_ref
  1.5 1.7 copy-done.2
  3.2 0.9 copy-done.9
  4.2 3.5 %analyse.1 = bf16[8,320,128]{2,1,0:T(8,128)(2,1)} custom-call(bf16[20,2,4,32,256]{4,3,2,1,0:T(8,128)(2,1)S(1)} %bitcast.14, bf16[2,256,256]{2,1,0:T(8,128)(2,1)S(1)} %copy-done.9, bf16[128,256]{1,0:T(8,128)(2,1)S(1)} %dynamic-slice_bitcast_fusion.1.table_ref), custom_call_target="tpu_custom_call" | custom-call | flops 671088640 | bytes 3145728 | tf_op jit(solution)/shard_map/analyse/pallas_call | solution.py:153
  7.7 0.6 copy-done.7
  8.3 5.9 %all-to-all-start = ((bf16[8,320,128]{2,1,0:T(8,128)(2,1)}), bf16[8,320,128]{2,1,0:T(8,128)(2,1)S(1)}, u32[]{:S(2)}, u32[]{:S(2)}) async-start(bf16[8,320,128]{2,1,0:T(8,128)(2,1)} %analyse.1), calls=%async_computation | async-start | bytes 1310720 | tf_op jit(solution)/shard_map/all_to_all | solution.py:509
  14.2 0.5 broadcast.3
  14.7 6.5 %reduce.3 = f32[2,20,20,4,32]{4,3,2,1,0:T(4,128)S(1)} reduce(f32[2,20,20,4,32,1]{4,5,3,2,1,0:T(1,128)} %param.20, f32[]{:T(128)} %broadcast.3), dimensions={5}, to_apply=%param.20.reduce_sub_computation.3 | reduce | bytes 819204 | tf_op args[2]
  21.3 0.7 reshape.31.weight_ref
  22.1 1.0 weight_out.1
  23.0 1.2 all-to-all-done.in_ref
  24.3 4.5 %all-to-all-start.2 = ((bf16[8,16,960]{2,1,0:T(8,128)(2,1)}), bf16[8,16,960]{2,1,0:T(8,128)(2,1)S(1)}, u32[]{:S(2)}, u32[]{:S(2)}) async-start(bf16[8,16,960]{2,1,0:T(8,128)(2,1)} %weight_out.1), calls=%async_computation.2 | async-start | bytes 524288 | tf_op jit(solution)/shard_map/all_to_all | solution.py:509
  28.7 1.0 gather.2
  29.7 4.9 %all-to-all-done.2.in_ref = bf16[8,16,960]{2,1,0:T(8,128)(2,1)S(1)} async-done(((bf16[8,16,960]{2,1,0:T(8,128)(2,1)}), bf16[8,16,960]{2,1,0:T(8,128)(2,1)S(1)}, u32[]{:S(2)}, u32[]{:S(2)}) %all-to-all-start.2) | async-done | bytes 245792 | tf_op jit(solution)/shard_map/all_to_all | solution.py:509
  34.6 10.4 %all-to-all-start.1 = ((bf16[32,16,128]{2,1,0:T(8,128)(2,1)}), bf16[32,16,128]{2,1,0:T(8,128)(2,1)S(1)}, u32[]{:S(2)}, u32[]{:S(2)}) async-start(bf16[32,16,128]{2,1,0:T(8,128)(2,1)} %gather.2), calls=%async_computation.1 | async-start | bytes 262144 | tf_op jit(solution)/shard_map/all_to_all | solution.py:509
  45.0 0.2 weight_in.1.weight_ref
  45.3 11.7 %all-to-all-done.1.lines_ref = bf16[32,16,128]{2,1,0:T(8,128)(2,1)S(1)} async-done(((bf16[32,16,128]{2,1,0:T(8,128)(2,1)}), bf16[32,16,128]{2,1,0:T(8,128)(2,1)S(1)}, u32[]{:S(2)}, u32[]{:S(2)}) %all-to-all-start.1) | async-done | bytes 131104 | tf_op jit(solution)/shard_map/all_to_all | solution.py:509
  57.0 0.6 mix.1
  57.5 0.6 copy-done.13
  58.1 15.0 %all_to_all.50.in_ref = bf16[32,16,128]{2,1,0:T(8,128)(2,1)S(1)} all-to-all(bf16[32,16,128]{2,1,0:T(8,128)(2,1)S(1)} %get-tuple-element.10), channel_id=1, replica_groups=mesh['wide'=32,'narrow'=8] {'wide'}, dimensions={0} | all-to-all | bytes 262144 | tf_op jit(solution)/shard_map/all_to_all | solution.py:509
  73.2 0.3 scatter.2
  73.5 0.8 copy-done.4
  74.3 6.1 %all-to-all-start.4 = ((bf16[8,320,128]{2,1,0:T(8,128)(2,1)}), bf16[8,320,128]{2,1,0:T(8,128)(2,1)}, u32[]{:S(2)}, u32[]{:S(2)}) async-start(bf16[8,320,128]{2,1,0:T(8,128)(2,1)} %copy-done.4), calls=%async_computation.4 | async-start | bytes 1310720 | tf_op jit(solution)/shard_map/all_to_all | solution.py:509
  80.4 2.1 %convolution_multiply_fusion = bf16[320,320]{0,1:T(8,128)(2,1)} fusion(bf16[320,320]{0,1:T(8,128)(2,1)} %constant.39.clone, bf16[320,20]{1,0:T(8,128)(2,1)} %constant.38.clone, bf16[20,20]{1,0:T(8,128)(2,1)S(1)} %copy-done), kind=kOutput, calls=%fused_computation | convolution fusion | flops 4761600 | bytes 423200 | tf_op jit(solution)/shard_map/dot_general | solution.py:530
  82.5 1.8 copy.27.local_ref
  84.4 0.1 broadcast_in_dim.11
  84.5 0.8 dynamic-slice_bitcast_fusion.inverse_ref
  85.3 4.6 %all-to-all-done.4.parts_ref = bf16[8,320,128]{2,1,0:T(8,128)(2,1)} async-done(((bf16[8,320,128]{2,1,0:T(8,128)(2,1)}), bf16[8,320,128]{2,1,0:T(8,128)(2,1)}, u32[]{:S(2)}, u32[]{:S(2)}) %all-to-all-start.4) | async-done | bytes 655392 | tf_op jit(solution)/shard_map/all_to_all | solution.py:509
  89.9 0.1 broadcast_in_dim.12.bias_ref
  90.0 0.9 copy-done.10
  91.0 1.7 copy-done.15
  92.7 0.9 copy-done.16
  93.7 0.9 copy-done.18
  94.6 10.5 %local.1 = (bf16[20,2,4,32,256]{4,3,2,1,0:T(8,128)(2,1)}, bf16[20,2,4,32,256]{4,3,2,1,0:T(8,128)(2,1)S(1)}, bf16[8,320,128]{2,1,0:T(8,128)(2,1)S(1)}) custom-call(bf16[8,320,128]{2,1,0:T(8,128)(2,1)} %all-to-all-done.4.parts_ref, bf16[20,2,4,32,256]{4,3,2,1,0:T(8,128)(2,1)S(1)} %bitcast.15, bf16[20,2,4,32,256]{4,3,2,1,0:T(8,128)(2,1)S(1)} %bitcast.17, ...), custom_call_target="tpu_custom_call" | custom-call | flops 3000000000 | bytes 12582912 | tf_op jit(solution)/shard_map/local/pallas_call | solution.py:447
  105.1 13.9 %all_to_all.51.in_ref = bf16[8,320,128]{2,1,0:T(8,128)(2,1)S(1)} all-to-all(bf16[8,320,128]{2,1,0:T(8,128)(2,1)S(1)} %get-tuple-element.12), channel_id=1, replica_groups=mesh['wide'=32,'narrow'=8] {'narrow'}, dimensions={0} | all-to-all | bytes 1310720 | tf_op jit(solution)/shard_map/all_to_all | solution.py:509
  119.0 0.3 gather.3
  119.3 15.4 %all_to_all.52.lines_ref = bf16[32,16,128]{2,1,0:T(8,128)(2,1)S(1)} all-to-all(bf16[32,16,128]{2,1,0:T(8,128)(2,1)S(1)} %gather.3), channel_id=1, replica_groups=mesh['wide'=32,'narrow'=8] {'wide'}, dimensions={0} | all-to-all | bytes 262144 | tf_op jit(solution)/shard_map/all_to_all | solution.py:509
  134.7 1.0 mix_back.1
  135.8 15.0 %all_to_all.53.in_ref = bf16[32,16,128]{2,1,0:T(8,128)(2,1)S(1)} all-to-all(bf16[32,16,128]{2,1,0:T(8,128)(2,1)S(1)} %get-tuple-element.14), channel_id=1, replica_groups=mesh['wide'=32,'narrow'=8] {'wide'}, dimensions={0} | all-to-all | bytes 262144 | tf_op jit(solution)/shard_map/all_to_all | solution.py:509
  150.8 4.8 %all-to-all-start.9 = ((bf16[8,16,128]{2,1,0:T(8,128)(2,1)}), bf16[8,16,128]{2,1,0:T(8,128)(2,1)S(1)}, u32[]{:S(2)}, u32[]{:S(2)}) async-start(bf16[8,16,128]{2,1,0:T(8,128)(2,1)} %get-tuple-element.16), calls=%async_computation.9 | async-start | bytes 65536 | tf_op jit(solution)/shard_map/all_to_all | solution.py:509
  155.6 1.1 scatter.3
  156.7 3.7 %all-to-all-done.9.pair_ref = bf16[8,16,128]{2,1,0:T(8,128)(2,1)S(1)} async-done(((bf16[8,16,128]{2,1,0:T(8,128)(2,1)}), bf16[8,16,128]{2,1,0:T(8,128)(2,1)S(1)}, u32[]{:S(2)}, u32[]{:S(2)}) %all-to-all-start.9) | async-done | bytes 32800 | tf_op jit(solution)/shard_map/all_to_all | solution.py:509
  160.4 4.9 %all-to-all-start.8 = ((bf16[8,320,128]{2,1,0:T(8,128)(2,1)}), bf16[8,320,128]{2,1,0:T(8,128)(2,1)S(1)}, u32[]{:S(2)}, u32[]{:S(2)}) async-start(bf16[8,320,128]{2,1,0:T(8,128)(2,1)} %scatter.3), calls=%async_computation.8 | async-start | bytes 1310720 | tf_op jit(solution)/shard_map/all_to_all | solution.py:509
  165.3 0.2 outer.1
  165.6 1.9 %reshape.32 = f32[2,20,20,4,32,1]{4,3,2,1,0,5:T(4,128)} reshape(f32[2,20,20,128]{3,2,1,0:T(8,128)S(1)} %outer.1) | data formatting | bytes 819200 | tf_op jit(solution)/shard_map/reshape | solution.py:568
  167.5 6.1 %all-to-all-done.8.parts_ref = bf16[8,320,128]{2,1,0:T(8,128)(2,1)S(1)} async-done(((bf16[8,320,128]{2,1,0:T(8,128)(2,1)}), bf16[8,320,128]{2,1,0:T(8,128)(2,1)S(1)}, u32[]{:S(2)}, u32[]{:S(2)}) %all-to-all-start.8) | async-done | bytes 655392 | tf_op jit(solution)/shard_map/all_to_all | solution.py:509
  173.6 1.7 copy-done.20
  175.3 5.7 %local_back.1 = bf16[20,2,4,32,256]{4,3,2,1,0:T(8,128)(2,1)} custom-call(bf16[8,320,128]{2,1,0:T(8,128)(2,1)S(1)} %all-to-all-done.8.parts_ref, bf16[20,2,4,32,256]{4,3,2,1,0:T(8,128)(2,1)S(1)} %copy-done.20, bf16[256,128]{1,0:T(8,128)(2,1)S(1)} %dynamic-slice_bitcast_fusion.inverse_ref, bf16[128,512]{1,0:T(8,128)(2,1)S(1)} %copy-done.17, ...), custom_call_target="tpu_custom_call" | custom-call | flops 2000000000 | bytes 6291456 | tf_op jit(solution)/shard_map/local_back/pallas_call | solution.py:489
  (35 shorter events, 0.2 us)
Async XLA Ops:
  0.6 79.8 %copy-start = (bf16[20,20]{1,0:T(8,128)(2,1)S(1)}, bf16[20,20]{1,0:T(8,128)(2,1)}, u32[]{:S(2)}) copy-start(bf16[20,20]{1,0:T(8,128)(2,1)} %param.21) | copy-start | bytes 2404
  1.5 1.7 copy-start.2
  3.2 0.9 copy-start.9
  7.7 0.6 copy-start.7
  8.3 16.0 %all-to-all-start = ((bf16[8,320,128]{2,1,0:T(8,128)(2,1)}), bf16[8,320,128]{2,1,0:T(8,128)(2,1)S(1)}, u32[]{:S(2)}, u32[]{:S(2)}) async-start(bf16[8,320,128]{2,1,0:T(8,128)(2,1)} %analyse.1), calls=%async_computation | async-start | bytes 1310720 | tf_op jit(solution)/shard_map/all_to_all | solution.py:509
  14.7 7.3 %copy-start.5 = (bf16[128,128]{1,0:T(8,128)(2,1)S(1)}, bf16[128,128]{1,0:T(8,128)(2,1)}, u32[]{:S(2)}) copy-start(bf16[128,128]{1,0:T(8,128)(2,1)} %constant.40.clone.perm_ref) | copy-start | bytes 98308
  21.3 23.7 %copy-start.11 = (bf16[128,128]{1,0:T(8,128)(2,1)S(1)}, bf16[128,128]{1,0:T(8,128)(2,1)}, u32[]{:S(2)}) copy-start(bf16[128,128]{1,0:T(8,128)(2,1)} %constant.41.clone.perm_ref) | copy-start | bytes 98308
  21.3 35.7 %copy-start.1 = (bf16[512,256]{1,0:T(8,128)(2,1)S(1)}, bf16[512,256]{1,0:T(8,128)(2,1)}, u32[]{:S(2)}) copy-start(bf16[512,256]{1,0:T(8,128)(2,1)} %constant.43.clone.first_ref.inverse_ref) | copy-start | bytes 786436
  24.3 10.3 %all-to-all-start.2 = ((bf16[8,16,960]{2,1,0:T(8,128)(2,1)}), bf16[8,16,960]{2,1,0:T(8,128)(2,1)S(1)}, u32[]{:S(2)}, u32[]{:S(2)}) async-start(bf16[8,16,960]{2,1,0:T(8,128)(2,1)} %weight_out.1), calls=%async_computation.2 | async-start | bytes 524288 | tf_op jit(solution)/shard_map/all_to_all | solution.py:509
  34.6 22.4 %all-to-all-start.1 = ((bf16[32,16,128]{2,1,0:T(8,128)(2,1)}), bf16[32,16,128]{2,1,0:T(8,128)(2,1)S(1)}, u32[]{:S(2)}, u32[]{:S(2)}) async-start(bf16[32,16,128]{2,1,0:T(8,128)(2,1)} %gather.2), calls=%async_computation.1 | async-start | bytes 262144 | tf_op jit(solution)/shard_map/all_to_all | solution.py:509
  45.0 39.3 %copy-start.21 = (f32[20]{0:T(128)S(1)}, f32[20]{0:T(128)}, u32[]{:S(2)}) copy-start(f32[20]{0:T(128)} %param.22) | copy-start | bytes 244
  45.3 44.7 %copy-start.3 = (bf16[20,8,32,256]{3,2,1,0:T(8,128)(2,1)S(1)}, bf16[20,8,32,256]{3,2,1,0:T(8,128)(2,1)}, u32[]{:S(2)}) copy-start(bf16[20,8,32,256]{3,2,1,0:T(8,128)(2,1)} %param.18) | copy-start | bytes 7864324
  57.5 0.6 copy-start.13
  58.1 31.9 %copy-start.8 = (bf16[128,256]{1,0:T(8,128)(2,1)S(1)}, bf16[128,256]{1,0:T(8,128)(2,1)}, u32[]{:S(2)}) copy-start(bf16[128,256]{1,0:T(8,128)(2,1)} %copy-done.7) | copy-start | bytes 196612
  73.5 0.8 copy-start.4
  74.3 15.6 %all-to-all-start.4 = ((bf16[8,320,128]{2,1,0:T(8,128)(2,1)}), bf16[8,320,128]{2,1,0:T(8,128)(2,1)}, u32[]{:S(2)}, u32[]{:S(2)}) async-start(bf16[8,320,128]{2,1,0:T(8,128)(2,1)} %copy-done.4), calls=%async_computation.4 | async-start | bytes 1310720 | tf_op jit(solution)/shard_map/all_to_all | solution.py:509
  90.0 0.9 copy-start.10
  91.0 1.7 copy-start.15
  92.7 0.9 copy-start.16
  93.7 0.9 copy-start.18
  94.6 40.2 %copy-start.12 = (bf16[128,128]{1,0:T(8,128)(2,1)S(1)}, bf16[128,128]{1,0:T(8,128)(2,1)}, u32[]{:S(2)}) copy-start(bf16[128,128]{1,0:T(8,128)(2,1)} %constant.41.clone.perm_ref) | copy-start | bytes 98308
  94.6 40.2 %copy-start.14 = (f32[2,32,128]{2,1,0:T(8,128)S(1)}, f32[2,32,128]{2,1,0:T(8,128)}, u32[]{:S(2)}) copy-start(f32[2,32,128]{2,1,0:T(8,128)} %copy-done.13) | copy-start | bytes 98308
  105.1 45.8 %copy-start.19 = (bf16[20,2,4,32,256]{4,3,2,1,0:T(8,128)(2,1)}, bf16[20,2,4,32,256]{4,3,2,1,0:T(8,128)(2,1)S(1)}, u32[]{:S(2)}) copy-start(bf16[20,2,4,32,256]{4,3,2,1,0:T(8,128)(2,1)S(1)} %get-tuple-element.15.slope_ref) | copy-start | bytes 7864324
  135.8 37.8 %copy-start.6 = (bf16[320,320]{0,1:T(8,128)(2,1)S(1)}, bf16[320,320]{0,1:T(8,128)(2,1)}, u32[]{:S(2)}) copy-start(bf16[320,320]{0,1:T(8,128)(2,1)} %convolution_multiply_fusion) | copy-start | bytes 614404
  135.8 37.8 %copy-start.17 = (bf16[128,512]{1,0:T(8,128)(2,1)S(1)}, bf16[128,512]{1,0:T(8,128)(2,1)}, u32[]{:S(2)}) copy-start(bf16[128,512]{1,0:T(8,128)(2,1)} %constant.46.clone.synth_ref) | copy-start | bytes 393220
  150.8 9.6 %all-to-all-start.9 = ((bf16[8,16,128]{2,1,0:T(8,128)(2,1)}), bf16[8,16,128]{2,1,0:T(8,128)(2,1)S(1)}, u32[]{:S(2)}, u32[]{:S(2)}) async-start(bf16[8,16,128]{2,1,0:T(8,128)(2,1)} %get-tuple-element.16), calls=%async_computation.9 | async-start | bytes 65536 | tf_op jit(solution)/shard_map/all_to_all | solution.py:509
  160.4 13.1 %all-to-all-start.8 = ((bf16[8,320,128]{2,1,0:T(8,128)(2,1)}), bf16[8,320,128]{2,1,0:T(8,128)(2,1)S(1)}, u32[]{:S(2)}, u32[]{:S(2)}) async-start(bf16[8,320,128]{2,1,0:T(8,128)(2,1)} %scatter.3), calls=%async_computation.8 | async-start | bytes 1310720 | tf_op jit(solution)/shard_map/all_to_all | solution.py:509
  173.6 1.7 copy-start.20
where the time goes:
time: 182 us; the launch traced here: 181 us
  blocking collectives  59.4 us (33%)
  starting transfers between devices  36.5 us (20%)
  waiting for transfers between devices  32.1 us (18%)
  Pallas kernels  25.5 us (14%)
  local copies, waits for them, and re-layouts  18 us (10%)
  other arithmetic  6.54 us (4%)
  matrix products  2.12 us (1%)
    all_to_all x4, blocking collectives, exchange(): return lax.all_to_all(value, axis, split_axis=0, concat_axis=0, tiled=True)  59.4 us
    all_to_all x6, starting transfers between devices, exchange(): return lax.all_to_all(value, axis, split_axis=0, concat_axis=0, tiled=True)  36.5 us
    all_to_all x6, waiting for transfers between devices, exchange(): return lax.all_to_all(value, axis, split_axis=0, concat_axis=0, tiled=True)  32.1 us
    unnamed x45, local copies, waits for them, and re-layouts  11.6 us
    pallas_call x1, Pallas kernels, local(): pl.pallas_call(local_kernel, grid=(8,), in_specs=[whole((8, C * 16, 128))...  10.5 us
    unnamed x1, other arithmetic  6.54 us
    pallas_call x1, Pallas kernels, local_back(): pl.pallas_call(local_back_kernel, grid=(8,), in_specs=[whole((8, C * 16,...  5.72 us
  transfers between devices with their start and end apart: 6, of which 6 were waited for; matrix products, arithmetic and copies ran while one was open for 8% of the time, Pallas kernels for 2%

commit v1 on v0

v1 whole, which is shorter than its diff:
```python
import functools
import math

import jax
import jax.numpy as jnp
import ml_dtypes
import numpy as np
from jax import lax
from jax.experimental import pallas as pl
from jax.experimental.pallas import tpu as pltpu
from jax.sharding import PartitionSpec as P

N = 256
M = 32
C = 20
CP = 24
BF = jnp.bfloat16
F32 = jnp.float32
MIB = 1024 * 1024


def depth_tables():
    index = np.arange(N)
    freq = np.arange(M)
    angle = (2.0 * math.pi / N) * ((freq[:, None] * index[None, :]) % N)
    scale = 1.0 / math.sqrt(N)
    weights = np.where(freq == 0, 1.0, 2.0)[:, None]
    forward = (np.concatenate([np.cos(angle), -np.sin(angle)]) * scale).T
    inverse = np.concatenate([weights * np.cos(angle), -weights * np.sin(angle)]) * scale
    return forward, inverse


def lateral_angles():
    index = np.arange(N)
    base = np.arange(M)
    freq = np.where(base < M // 2, base, N - M + base)
    angle = (2.0 * math.pi / N) * ((freq[:, None] * index[None, :]) % N)
    scale = 1.0 / math.sqrt(N)
    return np.cos(angle) * scale, np.sin(angle) * scale


def bf16(array):
    return np.asarray(array, np.float32).astype(ml_dtypes.bfloat16).astype(np.float32)


def analysis_depth(table):
    out = np.zeros((2, N, 2, 2, 2, M))
    for half in range(2):
        real, imag = table[:, :M], table[:, M:]
        out[half, :, 0, 0, half] = real
        out[half, :, 0, 1, half] = imag
        out[half, :, 1, 0, half] = imag
        out[half, :, 1, 1, half] = -real
    return bf16(out.reshape(2, N, 256))


def synthesis_depth(table):
    out = np.zeros((2, 2, M, 2, N))
    for half in range(2):
        out[:, half, :, half] = table.reshape(2, M, N)
    return bf16(out.reshape(128, 512))


def second_tables():
    cosine, sine = lateral_angles()
    out = np.zeros((8, 8, 4, 4, 2, 4, M))
    for block in range(8):
        rows = slice(block * M, (block + 1) * M)
        for x in range(4):
            out[block, :, :, x, 0, x] = cosine[:, rows].reshape(8, 4, M)
            out[block, :, :, x, 1, x] = sine[:, rows].reshape(8, 4, M)
    out = out.reshape(8, 128, 256)
    return bf16(out), bf16(out.transpose(0, 2, 1))


def first_tables():
    cosine, sine = lateral_angles()
    cos_x = cosine.T.reshape(M, 8, M)
    sin_x = sine.T.reshape(M, 8, M)
    forward = np.zeros((M, 2, 8, 2, 4, M))
    inverse = np.zeros((M, 2, 8, 2, 4, M))
    for j in range(4):
        forward[:, 0, :, 0, j] = cos_x
        forward[:, 0, :, 1, j] = -sin_x
        forward[:, 1, :, 0, j] = sin_x
        forward[:, 1, :, 1, j] = cos_x
        inverse[:, 0, :, 0, j] = cos_x
        inverse[:, 0, :, 1, j] = -sin_x
        inverse[:, 1, :, 0, j] = sin_x
        inverse[:, 1, :, 1, j] = cos_x
    return bf16(forward.reshape(512, 256)), bf16(inverse.reshape(512, 256))


def permutation(rows, lanes, sizes):
    total = int(np.prod([sizes[d] for d in rows]))
    position = np.arange(total).reshape([sizes[d] for d in rows])
    order = position.transpose([rows.index(d) for d in lanes]).reshape(-1)
    out = np.zeros((total, total))
    out[order, np.arange(total)] = 1.0
    return bf16(out)


def dot(a, b):
    return jnp.dot(a, b, preferred_element_type=F32)


def dot_nt(a, b):
    return lax.dot_general(a, b, (((1,), (1,)), ((), ())), preferred_element_type=F32)


def dot_tn(a, b):
    return lax.dot_general(a, b, (((0,), (0,)), ((), ())), preferred_element_type=F32)


def params(limit=40):
    return pltpu.CompilerParams(vmem_limit_bytes=limit * MIB)


def cost(flops, bytes_accessed, transcendentals=0):
    return pl.CostEstimate(
        flops=flops, bytes_accessed=bytes_accessed, transcendentals=transcendentals
    )


def whole(shape):
    return pl.BlockSpec(shape, lambda t, n: (0,) * len(shape))


def own(shape):
    return pl.BlockSpec((None,) + shape, lambda t, n: (n[0],) + (0,) * len(shape))


def second_forward(planes_ref, table, out_ref, first, count):
    for c in range(0, count, 2):
        one = planes_ref[first + c]
        two = planes_ref[first + c + 1]
        stacked = jnp.concatenate(
            [
                jnp.concatenate([one[:, :128], two[:, :128]], axis=1),
                jnp.concatenate([one[:, 128:], two[:, 128:]], axis=1),
            ],
            axis=0,
        )
        got = dot(table, stacked).astype(BF)
        for q in range(2):
            out_ref[:, (c + q) * 16 : (c + q + 1) * 16, :] = got[
                :, q * 128 : (q + 1) * 128
            ].reshape(8, 16, 128)


PARTS = C * 16
PAIR = PARTS + 16
STEP = 4
STEPS = C // STEP
FIELD_ROWS = STEP * 16
CARRY_ROWS = FIELD_ROWS + 32


def in_hbm(*arrays):
    return [pltpu.with_memory_space_constraint(jnp.asarray(a), pltpu.HBM) for a in arrays]


def analyse_kernel(
    block_ref, field_ref, weight_ref, depth_ref, table_ref, perm_ref, out_ref, planes_ref, rows_ref
):
    del block_ref

    @pl.when(pl.program_id(0) == 0)
    def _():
        rows_ref[...] = jnp.zeros((4, 256, M), F32)

    low = field_ref[:, 0].reshape(STEP * 128, N)
    high = field_ref[:, 1].reshape(STEP * 128, N)
    planes = dot(low, depth_ref[0].astype(BF)) + dot(high, depth_ref[1].astype(BF))
    planes_ref[...] = planes.astype(BF).reshape(STEP, 128, N)
    second_forward(planes_ref, table_ref[...].astype(BF), out_ref, 0, STEP)
    got = jnp.zeros((128, 256), F32)
    for i in range(4):
        for q in range(8):
            rows_ref[i, q * CP : q * CP + C, :] = weight_ref[
                pl.ds(q * 4 * C + i, C, stride=4), :
            ]
        got = got + dot_nt(perm_ref[i].astype(BF), rows_ref[i].astype(BF))
    got = got.astype(BF)
    for b in range(2):
        out_ref[:, FIELD_ROWS + b * 16 : FIELD_ROWS + (b + 1) * 16, :] = got[
            :, b * 128 : (b + 1) * 128
        ].reshape(8, 16, 128)


def analyse(block, *operands):
    return pl.pallas_call(
        analyse_kernel,
        grid_spec=pltpu.PrefetchScalarGridSpec(
            num_scalar_prefetch=1,
            grid=(STEPS,),
            in_specs=[
                pl.BlockSpec((STEP, 2, 4, M, N), lambda t, n: (t, 0, 0, 0, 0)),
                pl.BlockSpec((32 * C, M), lambda t, n: (t, 0)),
                whole((2, N, 256)),
                own((128, 256)),
                whole((4, 128, M)),
            ],
            out_specs=pl.BlockSpec((8, CARRY_ROWS, 128), lambda t, n: (0, t, 0)),
            scratch_shapes=[pltpu.VMEM((STEP, 128, 256), BF), pltpu.VMEM((4, 256, M), F32)],
        ),
        out_shape=jax.ShapeDtypeStruct((8, STEPS * CARRY_ROWS, 128), BF),
        compiler_params=params(),
        cost_estimate=cost(2 * 20 * 256 * 256 * 256, 3 * MIB),
        name="analyse",
    )(block, *in_hbm(*operands))


def gather_kernel(stride, in_ref, perm_ref, out_ref, sum_ref, rows_ref, turned_ref):
    for t in range(STEPS):
        rows = slice(t * stride, t * stride + FIELD_ROWS)
        total = in_ref[0, rows].astype(F32)
        for source in range(1, 8):
            total = total + in_ref[source, rows].astype(F32)
        sum_ref[t * FIELD_ROWS : (t + 1) * FIELD_ROWS] = total
    sum_ref[C * 16 :] = jnp.zeros((64, 128), F32)
    rows_ref[...] = jnp.zeros((512, 128), F32)
    for x in range(4):
        for j in range(4):
            rows_ref[x * 128 + j * 32 : x * 128 + j * 32 + CP, :] = sum_ref[
                pl.ds(j * 4 + x, CP, stride=16), :
            ]
    got = dot_nt(perm_ref[...].astype(BF), rows_ref[...].astype(BF))
    for x in range(4):
        turned_ref[pl.ds(x, 128, stride=4), :] = got[:, x * 128 : (x + 1) * 128]
    out_ref[...] = turned_ref[...].astype(BF).reshape(32, 16, 128)


def gather(parts, perm, stride):
    return pl.pallas_call(
        functools.partial(gather_kernel, stride),
        out_shape=jax.ShapeDtypeStruct((32, 16, 128), BF),
        scratch_shapes=[
            pltpu.VMEM((C * 16 + 64, 128), F32),
            pltpu.VMEM((512, 128), F32),
            pltpu.VMEM((512, 128), F32),
        ],
        compiler_params=params(),
        cost_estimate=cost(2 * 128 * 128 * 512, MIB),
        name="gather",
    )(parts, perm)


def scatter_kernel(*refs):
    if len(refs) == 6:
        in_ref, perm_ref, pair_ref, out_ref, turned_ref, rows_ref = refs
        out_ref[:, PARTS:, :] = pair_ref[...]
    else:
        in_ref, perm_ref, out_ref, turned_ref, rows_ref = refs
    turned_ref[...] = in_ref[...].reshape(512, 128).astype(F32)
    for x in range(4):
        block = turned_ref[pl.ds(x, 128, stride=4), :].astype(BF)
        got = dot_tn(block, perm_ref[...].astype(BF))
        for j in range(4):
            rows_ref[pl.ds(j * 4 + x, CP, stride=16), :] = got[j * 32 : j * 32 + CP]
    value = rows_ref[0 : C * 16].astype(BF)
    for target in range(8):
        out_ref[target, :PARTS] = value


def scatter(lines, perm, *pair):
    return pl.pallas_call(
        scatter_kernel,
        out_shape=jax.ShapeDtypeStruct((8, PAIR if pair else PARTS, 128), BF),
        scratch_shapes=[
            pltpu.VMEM((512, 128), F32),
            pltpu.VMEM((CP * 16, 128), F32),
        ],
        compiler_params=params(),
        cost_estimate=cost(2 * 128 * 128 * 512, MIB),
        name="scatter",
    )(lines, perm, *pair)


def lane_group(shape):
    return lax.broadcasted_iota(jnp.int32, shape, 1) // M % 4


def to_modes(lines_ref, first_ref):
    got = dot_tn(lines_ref[...].reshape(512, 128), first_ref[...].astype(BF))
    group = lane_group((M, 256))
    out = jnp.zeros((M, 256), F32)
    for j in range(4):
        out = jnp.where(group == j, got[j * M : (j + 1) * M], out)
    return out[:, :128], out[:, 128:]


def from_modes(real, imag, inverse_ref, out_ref):
    both = jnp.concatenate([real, imag], axis=1)
    group = lane_group((M, 256))
    rows = [jnp.where(group == j, both, 0.0) for j in range(4)]
    stacked = jnp.concatenate(rows, axis=0).astype(BF)
    out_ref[...] = dot_nt(inverse_ref[...].astype(BF), stacked).astype(BF).reshape(32, 16, 128)


def weight_row(part, c):
    index = part * C + c
    return (index // 8) * 256 + (index % 8) * CP


def mix_kernel(lines_ref, weight_ref, first_ref, inverse_ref, out_ref, spectrum_ref):
    real, imag = to_modes(lines_ref, first_ref)
    spectrum_ref[0] = real
    spectrum_ref[1] = imag
    mixed_real = jnp.zeros((CP, 128), F32)
    mixed_imag = jnp.zeros((CP, 128), F32)
    for c in range(C):
        w0 = weight_ref[weight_row(0, c) : weight_row(0, c) + CP, :]
        w1 = weight_ref[weight_row(1, c) : weight_row(1, c) + CP, :]
        s0 = real[c : c + 1]
        s1 = imag[c : c + 1]
        mixed_real = mixed_real + s0 * w0 - s1 * w1
        mixed_imag = mixed_imag + s0 * w1 + s1 * w0
    pad = jnp.zeros((M - CP, 128), F32)
    from_modes(
        jnp.concatenate([mixed_real, pad]),
        jnp.concatenate([mixed_imag, pad]),
        inverse_ref,
        out_ref,
    )


def mix_back_kernel(
    lines_ref, weight_ref, first_ref, inverse_ref, spectrum_ref, perm_ref, out_ref, pair_ref, acc_ref
):
    real, imag = to_modes(lines_ref, first_ref)
    both = jnp.concatenate([spectrum_ref[0], spectrum_ref[1], real, imag], axis=0)
    pair_ref[...] = dot_nt(perm_ref[...].astype(BF), both.astype(BF)).astype(BF).reshape(8, 16, 128)
    r0 = real[:CP]
    r1 = imag[:CP]
    acc_ref[...] = jnp.zeros((2, M, 128), F32)
    for c in range(C):
        w0 = weight_ref[weight_row(0, c) : weight_row(0, c) + CP, :]
        w1 = weight_ref[weight_row(1, c) : weight_row(1, c) + CP, :]
        acc_ref[0, c : c + 1, :] = jnp.sum(r0 * w0 + r1 * w1, axis=0, keepdims=True)
        acc_ref[1, c : c + 1, :] = jnp.sum(r1 * w0 - r0 * w1, axis=0, keepdims=True)
    from_modes(acc_ref[0], acc_ref[1], inverse_ref, out_ref)


def mix(lines, weight, first, inverse):
    return pl.pallas_call(
        mix_kernel,
        out_shape=[
            jax.ShapeDtypeStruct((32, 16, 128), BF),
            jax.ShapeDtypeStruct((2, M, 128), F32),
        ],
        compiler_params=params(),
        cost_estimate=cost(4 * 512 * 128 * 256, 2 * MIB),
        name="mix",
    )(lines, weight, first, inverse)


def mix_back(lines, weight, first, inverse, spectrum, perm):
    return pl.pallas_call(
        mix_back_kernel,
        out_shape=[
            jax.ShapeDtypeStruct((32, 16, 128), BF),
            jax.ShapeDtypeStruct((8, 16, 128), BF),
        ],
        scratch_shapes=[pltpu.VMEM((2, M, 128), F32)],
        compiler_params=params(),
        cost_estimate=cost(4 * 512 * 128 * 256, 2 * MIB),
        name="mix_back",
    )(lines, weight, first, inverse, spectrum, perm)


def weight_in_kernel(in_ref, perm_ref, out_ref):
    perm = perm_ref[...].astype(BF)
    for b in range(2):
        start = FIELD_ROWS + b * 16
        rows = in_ref[:, start : start + 16, :].reshape(128, 128)
        out_ref[b * 128 : (b + 1) * 128] = dot_tn(rows, perm)


def weight_in(parts, perm):
    return pl.pallas_call(
        weight_in_kernel,
        grid=(STEPS,),
        in_specs=[
            pl.BlockSpec((8, CARRY_ROWS, 128), lambda t: (0, t, 0)),
            pl.BlockSpec((128, 128), lambda t: (0, 0)),
        ],
        out_specs=pl.BlockSpec((256, 128), lambda t: (t, 0)),
        out_shape=jax.ShapeDtypeStruct((STEPS * 256, 128), F32),
        compiler_params=params(),
        cost_estimate=cost(2 * 128 * 128 * 1280, MIB),
        name="weight_in",
    )(parts, perm)


def second_inverse(in_ref, table_ref, planes_ref):
    table = table_ref[...].astype(BF)
    lane = lax.broadcasted_iota(jnp.int32, (128, 256), 1) % 128
    for c in range(0, C, 2):
        both = jnp.concatenate(
            [in_ref[:, (c + q) * 16 : (c + q + 1) * 16, :].reshape(128, 128) for q in range(2)],
            axis=1,
        )
        got = dot(table, both)
        for q in range(2):
            cos_part = got[:128, q * 128 : (q + 1) * 128]
            sin_part = got[128:, q * 128 : (q + 1) * 128]
            turned = pltpu.roll(sin_part, 64, 1)
            value = jnp.where(lane[:, :128] < 64, cos_part - turned, cos_part + turned)
            planes_ref[c + q] = value.astype(BF)


GRID_BLOCK = (C, 2, None, 16, N)
GRID = (C, 2, 4, M, N)


def grid_spec():
    return pl.BlockSpec(GRID_BLOCK, lambda t, *n: (0, 0, t // 2, t % 2, 0))


def widen(local_ref, spread_ref, same_ref, transposed):
    spread = spread_ref[...].astype(BF)
    multiply = dot_nt if transposed else dot
    rows = multiply(spread, local_ref[...]).astype(BF)
    return (dot_nt(rows, spread) * same_ref[...]).astype(BF)


def channels_kernel(transposed, field_ref, local_ref, spread_ref, same_ref, *refs):
    out_ref, wide_ref = refs[-2:]

    @pl.when(pl.program_id(0) == 0)
    def _():
        wide_ref[...] = widen(local_ref, spread_ref, same_ref, transposed)

    for x in range(2):
        value = dot(wide_ref[...], field_ref[:, x].reshape(C * 16, N)).reshape(C, 16, N)
        if not transposed:
            value = value + refs[0][...]
        out_ref[:, x] = value.astype(BF)


def channels(field, transposed, *operands):
    def block(shape):
        return pl.BlockSpec(shape, lambda t: (0,) * len(shape))

    shapes = [(C, C), (C * 16, C), (C * 16, C * 16), (C, 1, N)]
    return pl.pallas_call(
        functools.partial(channels_kernel, transposed),
        grid=(8,),
        in_specs=[grid_spec()] + [block(s) for s in shapes[: len(operands)]],
        out_specs=grid_spec(),
        out_shape=jax.ShapeDtypeStruct(GRID, BF),
        scratch_shapes=[pltpu.VMEM((C * 16, C * 16), BF)],
        compiler_params=params(16),
        cost_estimate=cost(2 * 10**9, 6 * MIB),
        name="channels",
    )(field, *in_hbm(*operands))


def local_kernel(
    block_ref,
    parts_ref,
    mixed_ref,
    cotangent_ref,
    inverse_ref,
    synth_ref,
    depth_ref,
    table_ref,
    activated_ref,
    slope_ref,
    out_ref,
    planes_ref,
    turned_ref,
    synth_scratch,
    depth_scratch,
):
    del block_ref
    step = pl.program_id(0)

    @pl.when(step == 0)
    def _():
        synth_scratch[...] = synth_ref[...].astype(BF)
        depth_scratch[...] = depth_ref[...].reshape(2 * N, 256).astype(BF)
        second_inverse(parts_ref, inverse_ref, planes_ref)

    rows = pl.ds(pl.multiple_of(step * 16, 16), 16)
    planes = planes_ref[:, rows, :].reshape(C * 16, 128)
    spatial = dot(planes, synth_scratch[...])
    slopes = []
    scale = 0.7978845608028654
    cubic = scale * 0.044715
    for x in range(2):
        pieces = []
        for c in range(C):
            value = spatial[c * 16 : (c + 1) * 16, x * N : (x + 1) * N]
            value = value + mixed_ref[c, x].astype(F32)
            square = value * value
            tanh = jnp.tanh(value * (scale + cubic * square))
            half = 0.5 + 0.5 * tanh
            activated_ref[c, x] = (value * half).astype(BF)
            d_inner = (0.5 * scale) + (1.5 * cubic) * square
            d_gelu = half + value * ((1.0 - tanh * tanh) * d_inner)
            slope = (cotangent_ref[c, x].astype(F32) * d_gelu).astype(BF)
            slope_ref[c, x] = slope
            pieces.append(slope)
        slopes.append(jnp.concatenate(pieces, axis=0))
    response = dot(jnp.concatenate(slopes, axis=1), depth_scratch[...])
    turned_ref[:, rows, :] = response.astype(BF).reshape(C, 16, 256)

    @pl.when(step == pl.num_programs(0) - 1)
    def _():
        second_forward(turned_ref, table_ref[...].astype(BF), out_ref, 0, C)


def local(block, parts, mixed, *operands):
    grid_shape = jax.ShapeDtypeStruct(GRID, BF)
    return pl.pallas_call(
        local_kernel,
        grid_spec=pltpu.PrefetchScalarGridSpec(
            num_scalar_prefetch=1,
            grid=(8,),
            in_specs=[
                whole((8, PARTS, 128)),
                grid_spec(),
                grid_spec(),
                own((256, 128)),
                whole((128, 512)),
                whole((2, N, 256)),
                own((128, 256)),
            ],
            out_specs=[grid_spec(), grid_spec(), whole((8, PARTS, 128))],
            scratch_shapes=[
                pltpu.VMEM((C, 128, 128), BF),
                pltpu.VMEM((C, 128, 256), BF),
                pltpu.VMEM((128, 512), BF),
                pltpu.VMEM((2 * N, 256), BF),
            ],
        ),
        out_shape=[grid_shape, grid_shape, jax.ShapeDtypeStruct((8, PARTS, 128), BF)],
        compiler_params=params(),
        cost_estimate=cost(10**9, 12 * MIB, 1310720),
        name="local",
    )(block, parts, mixed, *in_hbm(*operands))


def local_back_kernel(
    block_ref,
    parts_ref,
    mixed_ref,
    inverse_ref,
    synth_ref,
    perm_ref,
    out_ref,
    grad_ref,
    planes_ref,
    modes_ref,
    synth_scratch,
):
    del block_ref
    step = pl.program_id(0)

    @pl.when(step == 0)
    def _():
        synth_scratch[...] = synth_ref[...].astype(BF)
        second_inverse(parts_ref, inverse_ref, planes_ref)
        pair = parts_ref[:, PARTS:, :].reshape(128, 128)
        for i in range(4):
            modes_ref[pl.ds(i, 128, stride=4), :] = dot_tn(pair, perm_ref[i].astype(BF))

    r0 = modes_ref[8 * M : 8 * M + 4 * C, :]
    r1 = modes_ref[12 * M : 12 * M + 4 * C, :]
    for q in range(5):
        c = step * 5 + q
        s0 = modes_ref[pl.ds(c * 4, 4), :]
        s1 = modes_ref[pl.ds(4 * M + c * 4, 4), :]
        s0 = jnp.concatenate([s0] * C, axis=0)
        s1 = jnp.concatenate([s1] * C, axis=0)
        grad_ref[0, q] = s0 * r0 + s1 * r1
        grad_ref[1, q] = s0 * r1 - s1 * r0

    for h in range(2):
        rows = pl.ds(pl.multiple_of(step * 32 + h * 16, 16), 16)
        planes = planes_ref[:, rows, :].reshape(C * 16, 128)
        spatial = dot(planes, synth_scratch[...])
        for x in range(2):
            for c in range(C):
                value = spatial[c * 16 : (c + 1) * 16, x * N : (x + 1) * N]
                value = value + mixed_ref[c, x, h * 16 : (h + 1) * 16].astype(F32)
                out_ref[c, x, h * 16 : (h + 1) * 16] = value.astype(BF)


def local_back(block, parts, mixed, *operands):
    rows = pl.BlockSpec((C, 2, None, M, N), lambda t, n: (0, 0, t, 0, 0))
    return pl.pallas_call(
        local_back_kernel,
        grid_spec=pltpu.PrefetchScalarGridSpec(
            num_scalar_prefetch=1,
            grid=(4,),
            in_specs=[
                whole((8, PAIR, 128)),
                rows,
                own((256, 128)),
                whole((128, 512)),
                whole((4, 128, M)),
            ],
            out_specs=[
                rows,
                pl.BlockSpec((2, 5, 4 * C, M), lambda t, n: (0, t, 0, 0)),
            ],
            scratch_shapes=[
                pltpu.VMEM((C, 128, 128), BF),
                pltpu.VMEM((512, M), F32),
                pltpu.VMEM((128, 512), BF),
            ],
        ),
        out_shape=[
            jax.ShapeDtypeStruct(GRID, BF),
            jax.ShapeDtypeStruct((2, C, 4 * C, M), F32),
        ],
        compiler_params=params(),
        cost_estimate=cost(2 * 10**9, 6 * MIB),
        name="local_back",
    )(block, parts, mixed, *in_hbm(*operands))


def exchange(value, axis):
    return lax.all_to_all(value, axis, split_axis=0, concat_axis=0, tiled=True)


def shards(field, cotangent, spectral_weight, local_weight, local_bias):
    forward, inverse = depth_tables()
    forward_b, inverse_b = analysis_depth(forward), analysis_depth(inverse.T)
    synth_f, synth_b = synthesis_depth(inverse), synthesis_depth(forward.T)
    second, second_back = second_tables()
    first, first_back = first_tables()
    block = lax.axis_index("narrow").astype(jnp.int32).reshape(1)

    sizes = {"s": 2, "p": 2, "k": 32, "J": 8, "j": 4, "i": 4}
    perm_line = permutation("ksp", "spk", sizes)
    perm_weight = permutation("Jji", "iJj", sizes)
    perm_modes = permutation("Jji", "jJi", sizes)
    spread = np.zeros((C * 16, C), np.float32)
    spread[np.arange(C * 16), np.arange(C * 16) // 16] = 1.0
    same = bf16(np.equal(np.arange(C * 16)[:, None] % 16, np.arange(C * 16)[None, :] % 16))
    bias = jnp.broadcast_to(local_bias[:, None, None], (C, 1, N))

    perm_grad = np.stack([perm_weight[:, i * M : (i + 1) * M] for i in range(4)])

    shape = field.shape
    grid_field = field.reshape(GRID)
    grid_cotangent = cotangent.reshape(GRID)

    weight = jnp.transpose(spectral_weight, (0, 1, 2, 3, 5, 4)).reshape(8 * C * C, M)
    parts = exchange(analyse(block, grid_field, weight, forward_b, second, perm_grad), "narrow")
    mixed = channels(*in_hbm(grid_field), False, local_weight, spread, same, bias)
    weight = weight_in(parts, perm_modes)
    lines = exchange(gather(parts, perm_line, CARRY_ROWS), "wide")
    lines, spectrum = mix(lines, weight, first, first_back)
    lines = exchange(lines, "wide")
    parts = exchange(scatter(lines, perm_line), "narrow")
    activated, slope, parts = local(
        block, parts, mixed, grid_cotangent, second_back, synth_f, inverse_b, second
    )
    parts = exchange(parts, "narrow")
    mixed = channels(slope, True, local_weight, spread, same)
    lines = exchange(gather(parts, perm_line, FIELD_ROWS), "wide")
    lines, pair = mix_back(lines, weight, first, first_back, spectrum, perm_modes)
    lines = exchange(lines, "wide")
    parts = exchange(scatter(lines, perm_line, pair), "narrow")
    field_grad, weight_grad = local_back(block, parts, mixed, second_back, synth_b, perm_grad)
    return (
        activated.reshape(shape),
        field_grad.reshape(shape),
        weight_grad.reshape(spectral_weight.shape),
    )


def solution(mesh):
    return jax.shard_map(
        shards,
        mesh=mesh,
        in_specs=(
            P(None, "wide", "narrow", None),
            P(None, "wide", "narrow", None),
            P(None, None, None, "narrow", None, "wide"),
            P(),
            P(),
        ),
        out_specs=(
            P(None, "wide", "narrow", None),
            P(None, "wide", "narrow", None),
            P(None, None, None, "narrow", None, "wide"),
        ),
        check_vma=False,
    )
```

time: 182 us -> 160 us (0.88)
  blocking collectives: 59.4 us -> 78.7 us
  waiting for transfers between devices: 32.1 us -> 14.6 us
  starting transfers between devices: 36.5 us -> 20.9 us
  Pallas kernels: 25.5 us -> 38 us
  local copies, waits for them, and re-layouts: 18 us -> 5.69 us
  other arithmetic: 6.54 us -> 0 us
  matrix products: 2.12 us -> 0 us
    all_to_all x4 -> x5, blocking collectives: 59.4 us -> 78.7 us  [exchange(): return lax.all_to_all(value, axis, split_axis=0, concat_axis=0, tiled=True)]
    all_to_all x6 -> x3, waiting for transfers between devices: 32.1 us -> 14.6 us  [exchange(): return lax.all_to_all(value, axis, split_axis=0, concat_axis=0, tiled=True)]
    all_to_all x6 -> x3, starting transfers between devices: 36.5 us -> 20.9 us  [exchange(): return lax.all_to_all(value, axis, split_axis=0, concat_axis=0, tiled=True)]
    pallas_call x10, Pallas kernels: 23.8 us -> 36.9 us  [the longest x2 11.4 us: channels(): pl.pallas_call(functools.partial(channels_kernel, transposed), grid=(8,),...]
    unnamed x45 -> x16, local copies, waits for them, and re-layouts: 11.6 us -> 5 us
    unnamed x1 -> x0, other arithmetic: 6.54 us -> none
    reshape x2 -> x0, local copies, waits for them, and re-layouts: 2.62 us -> none  [the longest x1 1.89 us: shards(): weight_grad.reshape(spectral_weight.shape)]
    dot_general x1 -> x0, matrix products: 2.12 us -> none  [shards(): wide_weight = jnp.dot(jnp.dot(spread, local_weight), spread.T) * same]
  transfers between devices with their start and end apart: 6 -> 3, of which waited for: 6 -> 3; matrix products, arithmetic and copies ran while one was open for 8% -> 0% of each run, Pallas kernels for 2% -> 8%
where the time goes in v1:
time: 160 us; the launch traced here: 159 us
  blocking collectives  78.7 us (49%)
  Pallas kernels  38 us (24%)
  starting transfers between devices  20.9 us (13%)
  waiting for transfers between devices  14.6 us (9%)
  local copies, waits for them, and re-layouts  5.69 us (4%)
    all_to_all x5, blocking collectives, exchange(): return lax.all_to_all(value, axis, split_axis=0, concat_axis=0, tiled=True)  78.7 us
    all_to_all x3, starting transfers between devices, exchange(): return lax.all_to_all(value, axis, split_axis=0, concat_axis=0, tiled=True)  20.9 us
    all_to_all x3, waiting for transfers between devices, exchange(): return lax.all_to_all(value, axis, split_axis=0, concat_axis=0, tiled=True)  14.6 us
    pallas_call x2, Pallas kernels, channels(): pl.pallas_call(functools.partial(channels_kernel, transposed), grid=(8,),...  11.4 us
    pallas_call x1, Pallas kernels, local(): pl.pallas_call(local_kernel, grid_spec=pltpu.PrefetchScalarGridSpec(num_s...  10.1 us
    pallas_call x1, Pallas kernels, analyse(): pl.pallas_call(analyse_kernel, grid_spec=pltpu.PrefetchScalarGridSpec(num...  5.95 us
    unnamed x16, local copies, waits for them, and re-layouts  5 us
    pallas_call x1, Pallas kernels, local_back(): pl.pallas_call(local_back_kernel, grid_spec=pltpu.PrefetchScalarGridSpec(...  4.82 us
  transfers between devices with their start and end apart: 3, of which 3 were waited for; matrix products, arithmetic and copies ran while one was open for 0% of the time, Pallas kernels for 8%

profile of v1, /device:TPU:2, one launch (start us, length us, event | category | flops | bytes accessed | tf_op | source)
XLA Modules:
  0.0 158.6 jit_solution(14154978561189519625)
XLA Ops:
  0.6 0.0 copy-start.3
  0.6 5.9 %analyse.1 = bf16[8,480,128]{2,1,0:T(8,128)(2,1)S(1)} custom-call(s32[1]{0:T(128)} %bitcast.block_ref, bf16[20,2,4,32,256]{4,3,2,1,0:T(8,128)(2,1)} %bitcast.9, f32[3200,32]{1,0:T(8,128)} %bitcast.12, f32[2,256,256]{2,1,0:T(8,128)} %constant.28.clone.depth_ref, f32[8,128,256]{2,1,0:T(8,128)} %constant.29.clone.table_ref, f32[4,128,32]{2,1,0:T(8,128)} %constant.30.clone.perm_ref), custom_call_target="tpu_custom_call" | custom-call | flops 671088640 | bytes 3145728 | tf_op jit(solution)/shard_map/analyse/pallas_call | solution.py:192
  6.6 0.0 copy-start.4
  6.6 0.0 copy-start
  6.6 19.5 %all_to_all.40.in_ref = bf16[8,480,128]{2,1,0:T(8,128)(2,1)S(1)} all-to-all(bf16[8,480,128]{2,1,0:T(8,128)(2,1)S(1)} %analyse.1), channel_id=1, replica_groups=mesh['wide'=32,'narrow'=8] {'narrow'}, dimensions={0} | all-to-all | bytes 1966080 | tf_op jit(solution)/shard_map/all_to_all | solution.py:627
  26.1 0.0 copy-done.3
  26.1 1.0 gather.2
  27.1 10.4 %all-to-all-start.1 = ((bf16[32,16,128]{2,1,0:T(8,128)(2,1)}), bf16[32,16,128]{2,1,0:T(8,128)(2,1)S(1)}, u32[]{:S(2)}, u32[]{:S(2)}) async-start(bf16[32,16,128]{2,1,0:T(8,128)(2,1)} %gather.2), calls=%async_computation.1 | async-start | bytes 262144 | tf_op jit(solution)/shard_map/all_to_all | solution.py:627
  37.5 0.0 copy-done.4
  37.5 0.0 copy-start.7
  37.5 1.1 weight_in.1.weight_ref
  38.6 10.8 %all-to-all-done.1.lines_ref = bf16[32,16,128]{2,1,0:T(8,128)(2,1)S(1)} async-done(((bf16[32,16,128]{2,1,0:T(8,128)(2,1)}), bf16[32,16,128]{2,1,0:T(8,128)(2,1)S(1)}, u32[]{:S(2)}, u32[]{:S(2)}) %all-to-all-start.1) | async-done | bytes 131104 | tf_op jit(solution)/shard_map/all_to_all | solution.py:627
  49.5 0.0 copy-done
  49.5 0.6 mix.1
  50.0 14.9 %all_to_all.41.refs_0_ = bf16[32,16,128]{2,1,0:T(8,128)(2,1)S(1)} all-to-all(bf16[32,16,128]{2,1,0:T(8,128)(2,1)S(1)} %get-tuple-element.12), channel_id=1, replica_groups=mesh['wide'=32,'narrow'=8] {'wide'}, dimensions={0} | all-to-all | bytes 262144 | tf_op jit(solution)/shard_map/all_to_all | solution.py:627
  65.0 1.1 scatter.2
  66.1 5.5 %all-to-all-start.3 = ((bf16[8,320,128]{2,1,0:T(8,128)(2,1)}), bf16[8,320,128]{2,1,0:T(8,128)(2,1)S(1)}, u32[]{:S(2)}, u32[]{:S(2)}) async-start(bf16[8,320,128]{2,1,0:T(8,128)(2,1)} %scatter.2), calls=%async_computation.3 | async-start | bytes 1310720 | tf_op jit(solution)/shard_map/all_to_all | solution.py:627
  71.6 0.0 copy-done.7
  71.6 0.7 broadcast_in_dim.2.refs_0_
  72.3 6.6 %channels.2.mixed_ref = bf16[20,2,4,32,256]{4,3,2,1,0:T(8,128)(2,1)S(1)} custom-call(bf16[20,2,4,32,256]{4,3,2,1,0:T(8,128)(2,1)} %bitcast.10, bf16[20,20]{1,0:T(8,128)(2,1)} %local_ref.3, f32[320,20]{1,0:T(8,128)} %constant.31.clone.spread_ref, f32[320,320]{1,0:T(8,128)} %constant.32.clone.same_ref, f32[20,1,256]{2,1,0:T(1,128)} %broadcast_in_dim.2.refs_0_), custom_call_target="tpu_custom_call" | custom-call | flops 2000000000 | bytes 6291456 | tf_op jit(solution)/shard_map/channels/pallas_call | solution.py:447
  78.9 0.0 copy-start.1
  78.9 1.5 copy-done.1
  80.4 0.6 all-to-all-done.3.parts_ref
  81.0 0.0 copy-start.2
  81.0 1.7 %copy-done.2 = bf16[20,2,4,32,256]{4,3,2,1,0:T(8,128)(2,1)S(1)} copy-done((bf16[20,2,4,32,256]{4,3,2,1,0:T(8,128)(2,1)S(1)}, bf16[20,2,4,32,256]{4,3,2,1,0:T(8,128)(2,1)}, u32[]{:S(2)}) %copy-start.2) | copy-done | bytes 2621464
  82.7 10.1 %local.1 = (bf16[20,2,4,32,256]{4,3,2,1,0:T(8,128)(2,1)}, bf16[20,2,4,32,256]{4,3,2,1,0:T(8,128)(2,1)S(1)}, bf16[8,320,128]{2,1,0:T(8,128)(2,1)S(1)}) custom-call(s32[1]{0:T(128)} %bitcast.block_ref, bf16[8,320,128]{2,1,0:T(8,128)(2,1)S(1)} %all-to-all-done.3.parts_ref, bf16[20,2,4,32,256]{4,3,2,1,0:T(8,128)(2,1)S(1)} %copy-done.2, ...), custom_call_target="tpu_custom_call" | custom-call | flops 1000000000 | bytes 12582912 | tf_op jit(solution)/shard_map/local/pallas_call | solution.py:517
  92.8 0.0 copy-start.5
  92.8 13.9 %all_to_all.42.in_ref = bf16[8,320,128]{2,1,0:T(8,128)(2,1)S(1)} all-to-all(bf16[8,320,128]{2,1,0:T(8,128)(2,1)S(1)} %get-tuple-element.14), channel_id=1, replica_groups=mesh['wide'=32,'narrow'=8] {'narrow'}, dimensions={0} | all-to-all | bytes 1310720 | tf_op jit(solution)/shard_map/all_to_all | solution.py:627
  106.7 0.3 gather.3
  107.1 15.4 %all_to_all.43.lines_ref = bf16[32,16,128]{2,1,0:T(8,128)(2,1)S(1)} all-to-all(bf16[32,16,128]{2,1,0:T(8,128)(2,1)S(1)} %gather.3), channel_id=1, replica_groups=mesh['wide'=32,'narrow'=8] {'wide'}, dimensions={0} | all-to-all | bytes 262144 | tf_op jit(solution)/shard_map/all_to_all | solution.py:627
  122.5 0.6 mix_back.1
  123.1 14.9 %all_to_all.44.refs_0_ = bf16[32,16,128]{2,1,0:T(8,128)(2,1)S(1)} all-to-all(bf16[32,16,128]{2,1,0:T(8,128)(2,1)S(1)} %get-tuple-element.16), channel_id=1, replica_groups=mesh['wide'=32,'narrow'=8] {'wide'}, dimensions={0} | all-to-all | bytes 262144 | tf_op jit(solution)/shard_map/all_to_all | solution.py:627
  138.0 0.0 copy-done.5
  138.0 1.1 scatter.3
  139.1 5.0 %all-to-all-start.7 = ((bf16[8,336,128]{2,1,0:T(8,128)(2,1)}), bf16[8,336,128]{2,1,0:T(8,128)(2,1)S(1)}, u32[]{:S(2)}, u32[]{:S(2)}) async-start(bf16[8,336,128]{2,1,0:T(8,128)(2,1)} %scatter.3), calls=%async_computation.7 | async-start | bytes 1376256 | tf_op jit(solution)/shard_map/all_to_all | solution.py:627
  144.1 0.0 copy-start.6
  144.1 1.7 %copy-done.6 = bf16[20,2,4,32,256]{4,3,2,1,0:T(8,128)(2,1)S(1)} copy-done((bf16[20,2,4,32,256]{4,3,2,1,0:T(8,128)(2,1)S(1)}, bf16[20,2,4,32,256]{4,3,2,1,0:T(8,128)(2,1)}, u32[]{:S(2)}) %copy-start.6) | copy-done | bytes 2621464
  145.8 4.8 %channels.3.mixed_ref = bf16[20,2,4,32,256]{4,3,2,1,0:T(8,128)(2,1)S(1)} custom-call(bf16[20,2,4,32,256]{4,3,2,1,0:T(8,128)(2,1)S(1)} %copy-done.6, bf16[20,20]{1,0:T(8,128)(2,1)} %local_ref.3, f32[320,20]{1,0:T(8,128)} %constant.31.clone.spread_ref, f32[320,320]{1,0:T(8,128)} %constant.32.clone.same_ref), custom_call_target="tpu_custom_call" | custom-call | flops 2000000000 | bytes 6291456 | tf_op jit(solution)/shard_map/channels/pallas_call | solution.py:447
  150.7 3.1 %all-to-all-done.7.parts_ref = bf16[8,336,128]{2,1,0:T(8,128)(2,1)S(1)} async-done(((bf16[8,336,128]{2,1,0:T(8,128)(2,1)}), bf16[8,336,128]{2,1,0:T(8,128)(2,1)S(1)}, u32[]{:S(2)}, u32[]{:S(2)}) %all-to-all-start.7) | async-done | bytes 688160 | tf_op jit(solution)/shard_map/all_to_all | solution.py:627
  153.8 4.8 %local_back.1 = (bf16[20,2,4,32,256]{4,3,2,1,0:T(8,128)(2,1)}, f32[2,20,80,32]{3,2,1,0:T(8,128)}) custom-call(s32[1]{0:T(128)} %bitcast.block_ref, bf16[8,336,128]{2,1,0:T(8,128)(2,1)S(1)} %all-to-all-done.7.parts_ref, bf16[20,2,4,32,256]{4,3,2,1,0:T(8,128)(2,1)S(1)} %channels.3.mixed_ref, f32[8,256,128]{2,1,0:T(8,128)} %constant.36.clone.inverse_ref, ...), custom_call_target="tpu_custom_call" | custom-call | flops 2000000000 | bytes 6291456 | tf_op jit(solution)/shard_map/local_back/pallas_call | solution.py:594
Async XLA Ops:
  0.6 25.5 %copy-start.3 = (f32[128,128]{1,0:T(8,128)S(1)}, f32[128,128]{1,0:T(8,128)}, u32[]{:S(2)}) copy-start(f32[128,128]{1,0:T(8,128)} %constant.34.clone.perm_ref.refs_1_) | copy-start | bytes 196612
  6.6 30.9 %copy-start.4 = (f32[128,128]{1,0:T(8,128)S(1)}, f32[128,128]{1,0:T(8,128)}, u32[]{:S(2)}) copy-start(f32[128,128]{1,0:T(8,128)} %constant.33.clone.perm_ref) | copy-start | bytes 196612
  6.6 42.9 %copy-start = (f32[512,256]{1,0:T(8,128)S(1)}, f32[512,256]{1,0:T(8,128)}, u32[]{:S(2)}) copy-start(f32[512,256]{1,0:T(8,128)} %constant.35.clone.first_ref.inverse_ref) | copy-start | bytes 1572868
  27.1 22.4 %all-to-all-start.1 = ((bf16[32,16,128]{2,1,0:T(8,128)(2,1)}), bf16[32,16,128]{2,1,0:T(8,128)(2,1)S(1)}, u32[]{:S(2)}, u32[]{:S(2)}) async-start(bf16[32,16,128]{2,1,0:T(8,128)(2,1)} %gather.2), calls=%async_computation.1 | async-start | bytes 262144 | tf_op jit(solution)/shard_map/all_to_all | solution.py:627
  37.5 34.1 %copy-start.7 = (f32[20]{0:T(128)S(1)}, f32[20]{0:T(128)}, u32[]{:S(2)}) copy-start(f32[20]{0:T(128)} %param.22) | copy-start | bytes 244
  66.1 14.9 %all-to-all-start.3 = ((bf16[8,320,128]{2,1,0:T(8,128)(2,1)}), bf16[8,320,128]{2,1,0:T(8,128)(2,1)S(1)}, u32[]{:S(2)}, u32[]{:S(2)}) async-start(bf16[8,320,128]{2,1,0:T(8,128)(2,1)} %scatter.2), calls=%async_computation.3 | async-start | bytes 1310720 | tf_op jit(solution)/shard_map/all_to_all | solution.py:627
  78.9 1.5 copy-start.1
  81.0 1.7 %copy-start.2 = (bf16[20,2,4,32,256]{4,3,2,1,0:T(8,128)(2,1)S(1)}, bf16[20,2,4,32,256]{4,3,2,1,0:T(8,128)(2,1)}, u32[]{:S(2)}) copy-start(bf16[20,2,4,32,256]{4,3,2,1,0:T(8,128)(2,1)} %copy-done.1) | copy-start | bytes 7864324
  92.8 45.2 %copy-start.5 = (bf16[20,2,4,32,256]{4,3,2,1,0:T(8,128)(2,1)}, bf16[20,2,4,32,256]{4,3,2,1,0:T(8,128)(2,1)S(1)}, u32[]{:S(2)}) copy-start(bf16[20,2,4,32,256]{4,3,2,1,0:T(8,128)(2,1)S(1)} %get-tuple-element.18.field_ref) | copy-start | bytes 7864324
  139.1 14.7 %all-to-all-start.7 = ((bf16[8,336,128]{2,1,0:T(8,128)(2,1)}), bf16[8,336,128]{2,1,0:T(8,128)(2,1)S(1)}, u32[]{:S(2)}, u32[]{:S(2)}) async-start(bf16[8,336,128]{2,1,0:T(8,128)(2,1)} %scatter.3), calls=%async_computation.7 | async-start | bytes 1376256 | tf_op jit(solution)/shard_map/all_to_all | solution.py:627
  144.1 1.7 %copy-start.6 = (bf16[20,2,4,32,256]{4,3,2,1,0:T(8,128)(2,1)S(1)}, bf16[20,2,4,32,256]{4,3,2,1,0:T(8,128)(2,1)}, u32[]{:S(2)}) copy-start(bf16[20,2,4,32,256]{4,3,2,1,0:T(8,128)(2,1)} %copy-done.5) | copy-start | bytes 7864324

commit v2 on v1

v2 whole, which is shorter than its diff:
```python
import functools
import math

import jax
import jax.numpy as jnp
import ml_dtypes
import numpy as np
from jax import lax
from jax.experimental import pallas as pl
from jax.experimental.pallas import tpu as pltpu
from jax.sharding import PartitionSpec as P

N = 256
M = 32
C = 20
CP = 24
BF = jnp.bfloat16
F32 = jnp.float32
MIB = 1024 * 1024


def depth_tables():
    index = np.arange(N)
    freq = np.arange(M)
    angle = (2.0 * math.pi / N) * ((freq[:, None] * index[None, :]) % N)
    scale = 1.0 / math.sqrt(N)
    weights = np.where(freq == 0, 1.0, 2.0)[:, None]
    forward = (np.concatenate([np.cos(angle), -np.sin(angle)]) * scale).T
    inverse = np.concatenate([weights * np.cos(angle), -weights * np.sin(angle)]) * scale
    return forward, inverse


def lateral_angles():
    index = np.arange(N)
    base = np.arange(M)
    freq = np.where(base < M // 2, base, N - M + base)
    angle = (2.0 * math.pi / N) * ((freq[:, None] * index[None, :]) % N)
    scale = 1.0 / math.sqrt(N)
    return np.cos(angle) * scale, np.sin(angle) * scale


def bf16(array):
    return np.asarray(array, np.float32).astype(ml_dtypes.bfloat16).astype(np.float32)


def analysis_depth(table):
    out = np.zeros((N, 2, 2, 2, M))
    real, imag = table[:, :M], table[:, M:]
    out[:, 0, 0, 0] = real
    out[:, 0, 1, 0] = imag
    out[:, 1, 0, 0] = imag
    out[:, 1, 1, 0] = -real
    return bf16(out.reshape(N, 256))


def spread_depth(table):
    return jnp.concatenate([table, pltpu.roll(table, M, 1)], axis=0).astype(BF)


def spread_synth(table):
    zero = jnp.zeros((M, N), F32)
    rows = []
    for part in range(2):
        piece = table[part * M : (part + 1) * M]
        rows.append(jnp.concatenate([piece, zero], axis=1))
        rows.append(jnp.concatenate([zero, piece], axis=1))
    return jnp.concatenate(rows, axis=0).astype(BF)


def second_tables():
    cosine, sine = lateral_angles()
    out = np.zeros((8, 8, 4, 4, 2, 4, M))
    for block in range(8):
        rows = slice(block * M, (block + 1) * M)
        for x in range(4):
            out[block, :, :, x, 0, x] = cosine[:, rows].reshape(8, 4, M)
            out[block, :, :, x, 1, x] = sine[:, rows].reshape(8, 4, M)
    out = out.reshape(8, 128, 256)
    return bf16(out), bf16(out.transpose(0, 2, 1))


def first_table():
    cosine, sine = lateral_angles()
    cos_x = cosine.T.reshape(M, 8, M).transpose(1, 0, 2)
    sin_x = sine.T.reshape(M, 8, M).transpose(1, 0, 2)
    out = np.zeros((8, M, 2, 2, 4, M))
    for j in range(4):
        out[:, :, 0, 0, j] = cos_x
        out[:, :, 0, 1, j] = -sin_x
        out[:, :, 1, 0, j] = sin_x
        out[:, :, 1, 1, j] = cos_x
    return bf16(out.reshape(512, 256))


def line_table():
    out = np.zeros((M, 2, 2, 2, 2, M))
    for k in range(M):
        for part in range(2):
            for x in range(2):
                out[k, part, x, part, x, k] = 1.0
    return bf16(out.reshape(64, 256))


def permutation(rows, lanes, sizes):
    total = int(np.prod([sizes[d] for d in rows]))
    position = np.arange(total).reshape([sizes[d] for d in rows])
    order = position.transpose([rows.index(d) for d in lanes]).reshape(-1)
    out = np.zeros((total, total))
    out[order, np.arange(total)] = 1.0
    return bf16(out)


def dot(a, b):
    return jnp.dot(a, b, preferred_element_type=F32)


def dot_nt(a, b):
    return lax.dot_general(a, b, (((1,), (1,)), ((), ())), preferred_element_type=F32)


def dot_tn(a, b):
    return lax.dot_general(a, b, (((0,), (0,)), ((), ())), preferred_element_type=F32)


def params(limit=40):
    return pltpu.CompilerParams(vmem_limit_bytes=limit * MIB)


def cost(flops, bytes_accessed, transcendentals=0):
    return pl.CostEstimate(
        flops=flops, bytes_accessed=bytes_accessed, transcendentals=transcendentals
    )


def whole(shape):
    return pl.BlockSpec(shape, lambda t, n: (0,) * len(shape))


def own(shape):
    return pl.BlockSpec((None,) + shape, lambda t, n: (n[0],) + (0,) * len(shape))


def second_forward(planes_ref, table, out_ref, first, count):
    for c in range(0, count, 2):
        one = planes_ref[first + c]
        two = planes_ref[first + c + 1]
        stacked = jnp.concatenate(
            [
                jnp.concatenate([one[:, :128], two[:, :128]], axis=1),
                jnp.concatenate([one[:, 128:], two[:, 128:]], axis=1),
            ],
            axis=0,
        )
        got = dot(table, stacked).astype(BF)
        for q in range(2):
            out_ref[:, (c + q) * 16 : (c + q + 1) * 16, :] = got[
                :, q * 128 : (q + 1) * 128
            ].reshape(8, 16, 128)


PARTS = C * 16
PAIR = PARTS + 16
STEP = 4
STEPS = C // STEP
FIELD_ROWS = STEP * 16
CARRY_ROWS = FIELD_ROWS + 32


def in_hbm(*arrays):
    return [pltpu.with_memory_space_constraint(jnp.asarray(a), pltpu.HBM) for a in arrays]


def analyse_kernel(
    block_ref,
    field_ref,
    weight_ref,
    depth_ref,
    table_ref,
    perm_ref,
    out_ref,
    planes_ref,
    rows_ref,
    depth_scratch,
):
    del block_ref

    @pl.when(pl.program_id(0) == 0)
    def _():
        rows_ref[...] = jnp.zeros((4, 256, M), F32)
        depth_scratch[...] = spread_depth(depth_ref[...])

    rows = jnp.concatenate([field_ref[:, x].reshape(STEP * 128, N) for x in range(2)], axis=1)
    planes_ref[...] = dot(rows, depth_scratch[...]).astype(BF).reshape(STEP, 128, N)
    second_forward(planes_ref, table_ref[...].astype(BF), out_ref, 0, STEP)
    got = jnp.zeros((128, 256), F32)
    for i in range(4):
        for q in range(8):
            rows_ref[i, q * CP : q * CP + C, :] = weight_ref[
                pl.ds(q * 4 * C + i, C, stride=4), :
            ]
        got = got + dot_nt(perm_ref[i].astype(BF), rows_ref[i].astype(BF))
    got = got.astype(BF)
    for b in range(2):
        out_ref[:, FIELD_ROWS + b * 16 : FIELD_ROWS + (b + 1) * 16, :] = got[
            :, b * 128 : (b + 1) * 128
        ].reshape(8, 16, 128)


def analyse(block, *operands):
    return pl.pallas_call(
        analyse_kernel,
        grid_spec=pltpu.PrefetchScalarGridSpec(
            num_scalar_prefetch=1,
            grid=(STEPS,),
            in_specs=[
                pl.BlockSpec((STEP, 2, 4, M, N), lambda t, n: (t, 0, 0, 0, 0)),
                pl.BlockSpec((32 * C, M), lambda t, n: (t, 0)),
                whole((N, 256)),
                own((128, 256)),
                whole((4, 128, M)),
            ],
            out_specs=pl.BlockSpec((8, CARRY_ROWS, 128), lambda t, n: (0, t, 0)),
            scratch_shapes=[
                pltpu.VMEM((STEP, 128, 256), BF),
                pltpu.VMEM((4, 256, M), F32),
                pltpu.VMEM((2 * N, 256), BF),
            ],
        ),
        out_shape=jax.ShapeDtypeStruct((8, STEPS * CARRY_ROWS, 128), BF),
        compiler_params=params(),
        cost_estimate=cost(2 * 20 * 256 * 256 * 256, 3 * MIB),
        name="analyse",
    )(block, *in_hbm(*operands))


def gather_kernel(stride, in_ref, perm_ref, out_ref, sum_ref, rows_ref):
    for t in range(STEPS):
        rows = slice(t * stride, t * stride + FIELD_ROWS)
        total = in_ref[0, rows].astype(F32)
        for source in range(1, 8):
            total = total + in_ref[source, rows].astype(F32)
        sum_ref[t * FIELD_ROWS : (t + 1) * FIELD_ROWS] = total
    rows_ref[...] = jnp.zeros((640, 256), BF)
    for x in range(4):
        rows = sum_ref[pl.ds(x, 80, stride=4), :].astype(BF)
        rows_ref[x * 80 : (x + 1) * 80, :128] = rows
        rows_ref[320 + x * 80 : 320 + (x + 1) * 80, 128:] = rows
    got = dot_nt(perm_ref[...].astype(BF), rows_ref[...])
    out_ref[...] = got.astype(BF).reshape(32, 2, 640)


def gather(parts, perm, stride):
    return pl.pallas_call(
        functools.partial(gather_kernel, stride),
        out_shape=jax.ShapeDtypeStruct((32, 2, 640), BF),
        scratch_shapes=[pltpu.VMEM((PARTS, 128), F32), pltpu.VMEM((640, 256), BF)],
        compiler_params=params(),
        cost_estimate=cost(2 * 128 * 128 * 512, MIB),
        name="gather",
    )(parts, perm)


def scatter_kernel(*refs):
    if len(refs) == 5:
        in_ref, perm_ref, pair_ref, out_ref, rows_ref = refs
        out_ref[:, PARTS:, :] = pair_ref[...]
    else:
        in_ref, perm_ref, out_ref, rows_ref = refs
    got = dot_tn(in_ref[...].reshape(64, 640), perm_ref[...].astype(BF))
    for x in range(4):
        rows_ref[pl.ds(x, 80, stride=4), :] = (
            got[x * 80 : (x + 1) * 80, :128] + got[320 + x * 80 : 320 + (x + 1) * 80, 128:]
        )
    value = rows_ref[...].astype(BF)
    for target in range(8):
        out_ref[target, :PARTS] = value


def scatter(lines, perm, *pair):
    return pl.pallas_call(
        scatter_kernel,
        out_shape=jax.ShapeDtypeStruct((8, PAIR if pair else PARTS, 128), BF),
        scratch_shapes=[pltpu.VMEM((PARTS, 128), F32)],
        compiler_params=params(),
        cost_estimate=cost(2 * 128 * 128 * 512, MIB),
        name="scatter",
    )(lines, perm, *pair)


def lane_group(shape):
    return lax.broadcasted_iota(jnp.int32, shape, 1) // M % 4


def to_modes(lines_ref, first, rows_ref):
    lines = lines_ref[...].reshape(64, 640).astype(F32).T.astype(BF)
    got = jnp.zeros((80, 256), F32)
    for x in range(8):
        got = got + dot(lines[x * 80 : (x + 1) * 80], first[x * 64 : (x + 1) * 64])
    group = lane_group((CP, 128))
    both = []
    for part in range(2):
        rows_ref[part, 0:80] = got[:, part * 128 : (part + 1) * 128]
        rows_ref[part, 80:] = jnp.zeros((16, 128), F32)
        out = jnp.zeros((CP, 128), F32)
        for j in range(4):
            out = jnp.where(group == j, rows_ref[part, pl.ds(j, CP, stride=4), :], out)
        both.append(jnp.concatenate([out, jnp.zeros((M - CP, 128), F32)], axis=0))
    return both


def from_modes(real, imag, first, rows_ref, lines_ref, out_ref):
    group = lane_group((CP, 128))
    for j in range(4):
        rows_ref[0, pl.ds(j, CP, stride=4), :] = jnp.where(group == j, real, 0.0)
        rows_ref[1, pl.ds(j, CP, stride=4), :] = jnp.where(group == j, imag, 0.0)
    both = jnp.concatenate([rows_ref[0, 0:80], rows_ref[1, 0:80]], axis=1)
    got = dot_nt(first, both.astype(BF))
    for x in range(8):
        lines_ref[:, x * 80 : (x + 1) * 80] = got[x * 64 : (x + 1) * 64]
    out_ref[...] = lines_ref[...].astype(BF).reshape(32, 2, 640)


def weight_row(part, c):
    index = part * C + c
    return (index // 8) * 256 + (index % 8) * CP


def mix_kernel(lines_ref, weight_ref, first_ref, out_ref, spectrum_ref, rows_ref, turned_ref):
    first = first_ref[...].astype(BF)
    real, imag = to_modes(lines_ref, first, rows_ref)
    spectrum_ref[0] = real
    spectrum_ref[1] = imag
    mixed_real = jnp.zeros((CP, 128), F32)
    mixed_imag = jnp.zeros((CP, 128), F32)
    for c in range(C):
        w0 = weight_ref[weight_row(0, c) : weight_row(0, c) + CP, :]
        w1 = weight_ref[weight_row(1, c) : weight_row(1, c) + CP, :]
        s0 = real[c : c + 1]
        s1 = imag[c : c + 1]
        mixed_real = mixed_real + s0 * w0 - s1 * w1
        mixed_imag = mixed_imag + s0 * w1 + s1 * w0
    from_modes(mixed_real, mixed_imag, first, rows_ref, turned_ref, out_ref)


def mix_back_kernel(
    lines_ref,
    weight_ref,
    first_ref,
    spectrum_ref,
    perm_ref,
    out_ref,
    pair_ref,
    acc_ref,
    rows_ref,
    turned_ref,
):
    first = first_ref[...].astype(BF)
    real, imag = to_modes(lines_ref, first, rows_ref)
    both = jnp.concatenate([spectrum_ref[0], spectrum_ref[1], real, imag], axis=0)
    pair_ref[...] = dot_nt(perm_ref[...].astype(BF), both.astype(BF)).astype(BF).reshape(8, 16, 128)
    r0 = real[:CP]
    r1 = imag[:CP]
    acc_ref[...] = jnp.zeros((2, CP, 128), F32)
    for c in range(C):
        w0 = weight_ref[weight_row(0, c) : weight_row(0, c) + CP, :]
        w1 = weight_ref[weight_row(1, c) : weight_row(1, c) + CP, :]
        acc_ref[0, c : c + 1, :] = jnp.sum(r0 * w0 + r1 * w1, axis=0, keepdims=True)
        acc_ref[1, c : c + 1, :] = jnp.sum(r1 * w0 - r0 * w1, axis=0, keepdims=True)
    from_modes(acc_ref[0], acc_ref[1], first, rows_ref, turned_ref, out_ref)


def mix(*operands):
    return pl.pallas_call(
        mix_kernel,
        out_shape=[
            jax.ShapeDtypeStruct((32, 2, 640), BF),
            jax.ShapeDtypeStruct((2, M, 128), F32),
        ],
        scratch_shapes=[pltpu.VMEM((2, 4 * CP, 128), F32), pltpu.VMEM((64, 640), F32)],
        compiler_params=params(),
        cost_estimate=cost(4 * 512 * 128 * 256, 2 * MIB),
        name="mix",
    )(*operands)


def mix_back(*operands):
    return pl.pallas_call(
        mix_back_kernel,
        out_shape=[
            jax.ShapeDtypeStruct((32, 2, 640), BF),
            jax.ShapeDtypeStruct((8, 16, 128), BF),
        ],
        scratch_shapes=[
            pltpu.VMEM((2, CP, 128), F32),
            pltpu.VMEM((2, 4 * CP, 128), F32),
            pltpu.VMEM((64, 640), F32),
        ],
        compiler_params=params(),
        cost_estimate=cost(4 * 512 * 128 * 256, 2 * MIB),
        name="mix_back",
    )(*operands)


def weight_in_kernel(in_ref, perm_ref, out_ref):
    perm = perm_ref[...].astype(BF)
    for b in range(2):
        start = FIELD_ROWS + b * 16
        rows = in_ref[:, start : start + 16, :].reshape(128, 128)
        out_ref[b * 128 : (b + 1) * 128] = dot_tn(rows, perm)


def weight_in(parts, perm):
    return pl.pallas_call(
        weight_in_kernel,
        grid=(STEPS,),
        in_specs=[
            pl.BlockSpec((8, CARRY_ROWS, 128), lambda t: (0, t, 0)),
            pl.BlockSpec((128, 128), lambda t: (0, 0)),
        ],
        out_specs=pl.BlockSpec((256, 128), lambda t: (t, 0)),
        out_shape=jax.ShapeDtypeStruct((STEPS * 256, 128), F32),
        compiler_params=params(),
        cost_estimate=cost(2 * 128 * 128 * 1280, MIB),
        name="weight_in",
    )(parts, perm)


def second_inverse(in_ref, table, planes_ref):
    lane = lax.broadcasted_iota(jnp.int32, (128, 256), 1) % 128
    for c in range(0, C, 2):
        both = jnp.concatenate(
            [in_ref[:, (c + q) * 16 : (c + q + 1) * 16, :].reshape(128, 128) for q in range(2)],
            axis=1,
        )
        got = dot(table, both)
        for q in range(2):
            cos_part = got[:128, q * 128 : (q + 1) * 128]
            sin_part = got[128:, q * 128 : (q + 1) * 128]
            turned = pltpu.roll(sin_part, 64, 1)
            value = jnp.where(lane[:, :128] < 64, cos_part - turned, cos_part + turned)
            planes_ref[c + q] = value.astype(BF)


GRID_BLOCK = (C, 2, None, 16, N)
GRID = (C, 2, 4, M, N)


def grid_spec():
    return pl.BlockSpec(GRID_BLOCK, lambda t, *n: (0, 0, t // 2, t % 2, 0))


def widen(local_ref, spread_ref, same_ref, transposed):
    spread = spread_ref[...].astype(BF)
    multiply = dot_nt if transposed else dot
    rows = multiply(spread, local_ref[...]).astype(BF)
    return (dot_nt(rows, spread) * same_ref[...]).astype(BF)


def channels_kernel(transposed, *refs):
    if transposed:
        _, field_ref, local_ref, spread_ref, same_ref, synth_ref, out_ref, synth_out, wide_ref = refs
    else:
        (
            _,
            field_ref,
            local_ref,
            spread_ref,
            same_ref,
            bias_ref,
            synth_ref,
            depth_ref,
            table_ref,
            inverse_ref,
            out_ref,
            synth_out,
            depth_out,
            table_out,
            inverse_out,
            wide_ref,
        ) = refs

    @pl.when(pl.program_id(0) == 0)
    def _():
        wide_ref[...] = widen(local_ref, spread_ref, same_ref, transposed)
        synth_out[...] = spread_synth(synth_ref[...])
        if not transposed:
            depth_out[...] = spread_depth(depth_ref[...])
            table_out[...] = table_ref[...].astype(BF)
            inverse_out[...] = inverse_ref[...].astype(BF)

    for x in range(2):
        value = dot(wide_ref[...], field_ref[:, x].reshape(C * 16, N)).reshape(C, 16, N)
        if not transposed:
            value = value + bias_ref[...]
        out_ref[:, x] = value.astype(BF)


def channels(block, transposed, *operands):
    grid_shape = pltpu.HBM(GRID, BF)
    mixing = [whole((C, C)), whole((C * 16, C)), whole((C * 16, C * 16))]
    synth = whole((2 * M, N))
    synth_out = whole((128, 512))
    synth_shape = jax.ShapeDtypeStruct((128, 512), BF)
    if transposed:
        in_specs = [grid_spec()] + mixing + [synth]
        out_specs = [grid_spec(), synth_out]
        out_shape = [grid_shape, synth_shape]
    else:
        in_specs = [grid_spec()] + mixing + [whole((C, 1, N)), synth]
        in_specs += [whole((N, 256)), own((128, 256)), own((256, 128))]
        out_specs = [grid_spec(), synth_out]
        out_specs += [whole((2 * N, 256)), whole((128, 256)), whole((256, 128))]
        out_shape = [grid_shape, synth_shape] + [
            jax.ShapeDtypeStruct(s, BF) for s in ((2 * N, 256), (128, 256), (256, 128))
        ]
    return pl.pallas_call(
        functools.partial(channels_kernel, transposed),
        grid_spec=pltpu.PrefetchScalarGridSpec(
            num_scalar_prefetch=1,
            grid=(8,),
            in_specs=in_specs,
            out_specs=out_specs,
            scratch_shapes=[pltpu.VMEM((C * 16, C * 16), BF)],
        ),
        out_shape=out_shape,
        compiler_params=params(16),
        cost_estimate=cost(2 * 10**9, 6 * MIB),
        name="channels",
    )(block, *operands)


def piece(ref, t):
    return ref.at[:, :, t // 2, pl.ds(pl.multiple_of((t % 2) * 16, 16), 16), :]


def moving(source, target, t, sem):
    return pltpu.make_async_copy(piece(source, t), piece(target, t), sem.at[t])


def local_kernel(
    parts_ref,
    mixed_hbm,
    cotangent_hbm,
    synth_ref,
    depth_ref,
    table_ref,
    inverse_ref,
    activated_hbm,
    slope_hbm,
    out_ref,
    planes_ref,
    turned_ref,
    mixed_ref,
    cotangent_ref,
    activated_ref,
    slope_ref,
    mixed_sem,
    cotangent_sem,
    activated_sem,
    slope_sem,
):
    for t in range(8):
        moving(mixed_hbm, mixed_ref, t, mixed_sem).start()
        moving(cotangent_hbm, cotangent_ref, t, cotangent_sem).start()
    second_inverse(parts_ref, inverse_ref[...], planes_ref)
    scale = 0.7978845608028654
    cubic = scale * 0.044715

    def step(t, carry):
        moving(mixed_hbm, mixed_ref, t, mixed_sem).wait()
        moving(cotangent_hbm, cotangent_ref, t, cotangent_sem).wait()
        y = pl.ds(pl.multiple_of((t % 2) * 16, 16), 16)
        rows = pl.ds(pl.multiple_of(t * 16, 16), 16)
        planes = planes_ref[:, rows, :].reshape(C * 16, 128)
        spatial = dot(planes, synth_ref[...])
        slopes = []
        for x in range(2):
            pieces = []
            for c in range(C):
                value = spatial[c * 16 : (c + 1) * 16, x * N : (x + 1) * N]
                value = value + mixed_ref[c, x, t // 2, y, :].astype(F32)
                square = value * value
                tanh = jnp.tanh(value * (scale + cubic * square))
                half = 0.5 + 0.5 * tanh
                activated_ref[c, x, t // 2, y, :] = (value * half).astype(BF)
                d_inner = (0.5 * scale) + (1.5 * cubic) * square
                d_gelu = half + value * ((1.0 - tanh * tanh) * d_inner)
                slope = (cotangent_ref[c, x, t // 2, y, :].astype(F32) * d_gelu).astype(BF)
                slope_ref[c, x, t // 2, y, :] = slope
                pieces.append(slope)
            slopes.append(jnp.concatenate(pieces, axis=0))
        moving(activated_ref, activated_hbm, t, activated_sem).start()
        moving(slope_ref, slope_hbm, t, slope_sem).start()
        response = dot(jnp.concatenate(slopes, axis=1), depth_ref[...])
        turned_ref[:, rows, :] = response.astype(BF).reshape(C, 16, 256)
        return carry

    lax.fori_loop(0, 8, step, 0)
    second_forward(turned_ref, table_ref[...], out_ref, 0, C)
    for t in range(8):
        moving(activated_ref, activated_hbm, t, activated_sem).wait()
        moving(slope_ref, slope_hbm, t, slope_sem).wait()


VMEM = pl.BlockSpec(memory_space=pltpu.VMEM)
HBM = pl.BlockSpec(memory_space=pltpu.HBM)


def local(parts, mixed, cotangent, *tables):
    grid_shape = pltpu.HBM(GRID, BF)
    return pl.pallas_call(
        local_kernel,
        in_specs=[VMEM, HBM, HBM] + [VMEM] * len(tables),
        out_specs=[HBM, HBM, VMEM],
        out_shape=[grid_shape, grid_shape, jax.ShapeDtypeStruct((8, PARTS, 128), BF)],
        scratch_shapes=[pltpu.VMEM((C, 128, 128), BF), pltpu.VMEM((C, 128, 256), BF)]
        + [pltpu.VMEM(GRID, BF)] * 4
        + [pltpu.SemaphoreType.DMA((8,))] * 4,
        compiler_params=params(24),
        cost_estimate=cost(10**9, 12 * MIB, 1310720),
        name="local",
    )(parts, *in_hbm(mixed, cotangent), *tables)


def local_back_kernel(
    parts_ref,
    mixed_hbm,
    synth_ref,
    inverse_ref,
    perm_ref,
    out_hbm,
    grad_hbm,
    planes_ref,
    modes_ref,
    mixed_ref,
    out_ref,
    grad_ref,
    mixed_sem,
    out_sem,
    grad_sem,
):
    for t in range(8):
        moving(mixed_hbm, mixed_ref, t, mixed_sem).start()

    pair = parts_ref[:, PARTS:, :].reshape(128, 128)
    for i in range(4):
        modes_ref[pl.ds(i, 128, stride=4), :] = dot_tn(pair, perm_ref[i].astype(BF))
    r0 = modes_ref[8 * M : 8 * M + 4 * C, :]
    r1 = modes_ref[12 * M : 12 * M + 4 * C, :]

    def outer(t):
        return pltpu.make_async_copy(
            grad_ref.at[:, pl.ds(t * 5, 5)], grad_hbm.at[:, pl.ds(t * 5, 5)], grad_sem.at[t]
        )

    for c in range(C):
        s0 = jnp.concatenate([modes_ref[c * 4 : c * 4 + 4, :]] * C, axis=0)
        s1 = jnp.concatenate([modes_ref[4 * M + c * 4 : 4 * M + c * 4 + 4, :]] * C, axis=0)
        grad_ref[0, c] = s0 * r0 + s1 * r1
        grad_ref[1, c] = s0 * r1 - s1 * r0
        if c % 5 == 4:
            outer(c // 5).start()

    second_inverse(parts_ref, inverse_ref[...], planes_ref)

    def step(t, carry):
        moving(mixed_hbm, mixed_ref, t, mixed_sem).wait()
        y = pl.ds(pl.multiple_of((t % 2) * 16, 16), 16)
        rows = pl.ds(pl.multiple_of(t * 16, 16), 16)
        planes = planes_ref[:, rows, :].reshape(C * 16, 128)
        spatial = dot(planes, synth_ref[...])
        for x in range(2):
            for c in range(C):
                value = spatial[c * 16 : (c + 1) * 16, x * N : (x + 1) * N]
                value = value + mixed_ref[c, x, t // 2, y, :].astype(F32)
                out_ref[c, x, t // 2, y, :] = value.astype(BF)
        moving(out_ref, out_hbm, t, out_sem).start()
        return carry

    lax.fori_loop(0, 8, step, 0)
    for t in range(8):
        moving(out_ref, out_hbm, t, out_sem).wait()
    for t in range(4):
        outer(t).wait()


def local_back(parts, mixed, *tables):
    grad = (2, C, 4 * C, M)
    return pl.pallas_call(
        local_back_kernel,
        in_specs=[VMEM, HBM] + [VMEM] * len(tables),
        out_specs=[HBM, HBM],
        out_shape=[pltpu.HBM(GRID, BF), pltpu.HBM(grad, F32)],
        scratch_shapes=[
            pltpu.VMEM((C, 128, 128), BF),
            pltpu.VMEM((512, M), F32),
            pltpu.VMEM(GRID, BF),
            pltpu.VMEM(GRID, BF),
            pltpu.VMEM(grad, F32),
            pltpu.SemaphoreType.DMA((8,)),
            pltpu.SemaphoreType.DMA((8,)),
            pltpu.SemaphoreType.DMA((4,)),
        ],
        compiler_params=params(24),
        cost_estimate=cost(2 * 10**9, 6 * MIB),
        name="local_back",
    )(parts, *in_hbm(mixed), *tables)


def exchange(value, axis):
    return lax.all_to_all(value, axis, split_axis=0, concat_axis=0, tiled=True)


def shards(field, cotangent, spectral_weight, local_weight, local_bias):
    forward, inverse = depth_tables()
    forward_b, inverse_b = analysis_depth(forward), analysis_depth(inverse.T)
    synth_f, synth_b = bf16(inverse), bf16(forward.T)
    second, second_back = second_tables()
    first = first_table()
    block = lax.axis_index("narrow").astype(jnp.int32).reshape(1)

    sizes = {"J": 8, "j": 4, "i": 4}
    perm_line = line_table()
    perm_weight = permutation("Jji", "iJj", sizes)
    perm_modes = permutation("Jji", "jJi", sizes)
    spread = np.zeros((C * 16, C), np.float32)
    spread[np.arange(C * 16), np.arange(C * 16) // 16] = 1.0
    same = bf16(np.equal(np.arange(C * 16)[:, None] % 16, np.arange(C * 16)[None, :] % 16))
    bias = jnp.broadcast_to(local_bias[:, None, None], (C, 1, N))

    perm_grad = np.stack([perm_weight[:, i * M : (i + 1) * M] for i in range(4)])

    shape = field.shape
    grid_field = field.reshape(GRID)
    grid_cotangent = cotangent.reshape(GRID)

    weight = jnp.transpose(spectral_weight, (0, 1, 2, 3, 5, 4)).reshape(8 * C * C, M)
    parts = exchange(analyse(block, grid_field, weight, forward_b, second, perm_grad), "narrow")
    mixed, synth, depth, table, table_back = channels(
        block,
        False,
        *in_hbm(grid_field, local_weight, spread, same, bias),
        *in_hbm(synth_f, inverse_b, second, second_back),
    )
    weight = weight_in(parts, perm_modes)
    lines = exchange(gather(parts, perm_line, CARRY_ROWS), "wide")
    lines, spectrum = mix(lines, weight, first)
    lines = exchange(lines, "wide")
    parts = exchange(scatter(lines, perm_line), "narrow")
    activated, slope, parts = local(
        parts, mixed, grid_cotangent, synth, depth, table, table_back
    )
    parts = exchange(parts, "narrow")
    mixed, synth = channels(
        block, True, *in_hbm(slope, local_weight, spread, same, synth_b)
    )
    lines = exchange(gather(parts, perm_line, FIELD_ROWS), "wide")
    lines, pair = mix_back(lines, weight, first, spectrum, perm_modes)
    lines = exchange(lines, "wide")
    parts = exchange(scatter(lines, perm_line, pair), "narrow")
    field_grad, weight_grad = local_back(parts, mixed, synth, table_back, perm_grad)
    return (
        activated.reshape(shape),
        field_grad.reshape(shape),
        weight_grad.reshape(spectral_weight.shape),
    )


def solution(mesh):
    return jax.shard_map(
        shards,
        mesh=mesh,
        in_specs=(
            P(None, "wide", "narrow", None),
            P(None, "wide", "narrow", None),
            P(None, None, None, "narrow", None, "wide"),
            P(),
            P(),
        ),
        out_specs=(
            P(None, "wide", "narrow", None),
            P(None, "wide", "narrow", None),
            P(None, None, None, "narrow", None, "wide"),
        ),
        check_vma=False,
    )
```

time: 160 us -> 153 us (0.956)
  local copies, waits for them, and re-layouts: 5.69 us -> 0.72 us
  blocking collectives: 78.7 us -> 75.5 us
  Pallas kernels: 38 us -> 41.1 us
    unnamed x16 -> x10, local copies, waits for them, and re-layouts: 5 us -> 0.03 us
    all_to_all x5, blocking collectives: 78.7 us -> 75.5 us  [exchange(): return lax.all_to_all(value, axis, split_axis=0, concat_axis=0, tiled=True)]
    pallas_call x6, Pallas kernels: 27.4 us -> 30.4 us  [the longest x2 15.5 us: channels(): pl.pallas_call(functools.partial(channels_kernel, transposed), grid_spec=...]
    all_to_all x3, waiting for transfers between devices: 14.6 us -> 13 us  [exchange(): return lax.all_to_all(value, axis, split_axis=0, concat_axis=0, tiled=True)]
  transfers between devices with their start and end apart: 3 -> 3, of which waited for: 3 -> 3; matrix products, arithmetic and copies ran while one was open for 0% -> 0% of each run, Pallas kernels for 8% -> 11%
where the time goes in v2:
time: 153 us; the launch traced here: 152 us
  blocking collectives  75.5 us (49%)
  Pallas kernels  41.1 us (27%)
  starting transfers between devices  20.8 us (14%)
  waiting for transfers between devices  13 us (8%)
    all_to_all x5, blocking collectives, exchange(): return lax.all_to_all(value, axis, split_axis=0, concat_axis=0, tiled=True)  75.5 us
    all_to_all x3, starting transfers between devices, exchange(): return lax.all_to_all(value, axis, split_axis=0, concat_axis=0, tiled=True)  20.8 us
    pallas_call x2, Pallas kernels, channels(): pl.pallas_call(functools.partial(channels_kernel, transposed), grid_spec=...  15.5 us
    all_to_all x3, waiting for transfers between devices, exchange(): return lax.all_to_all(value, axis, split_axis=0, concat_axis=0, tiled=True)  13 us
    pallas_call x1, Pallas kernels, local(): pl.pallas_call(local_kernel, in_specs=[VMEM, HBM, HBM] + [VMEM] * len(tab...  8.65 us
    pallas_call x1, Pallas kernels, analyse(): pl.pallas_call(analyse_kernel, grid_spec=pltpu.PrefetchScalarGridSpec(num...  5.93 us
    pallas_call x1, Pallas kernels, local_back(): pl.pallas_call(local_back_kernel, in_specs=[VMEM, HBM] + [VMEM] * len(tab...  4.54 us
  transfers between devices with their start and end apart: 3, of which 3 were waited for; matrix products, arithmetic and copies ran while one was open for 0% of the time, Pallas kernels for 11%

profile of v2, /device:TPU:2, one launch (start us, length us, event | category | flops | bytes accessed | tf_op | source)
XLA Modules:
  0.0 151.8 jit_solution(6158592053243259032)
XLA Ops:
  0.6 0.0 copy-start.1
  0.6 5.9 %analyse.1 = bf16[8,480,128]{2,1,0:T(8,128)(2,1)S(1)} custom-call(s32[1]{0:T(128)} %bitcast.block_ref.refs_0_, bf16[20,2,4,32,256]{4,3,2,1,0:T(8,128)(2,1)} %bitcast.10, f32[3200,32]{1,0:T(8,128)} %bitcast.12, f32[256,256]{1,0:T(8,128)} %constant.28.clone.depth_ref, f32[8,128,256]{2,1,0:T(8,128)} %constant.29.clone.table_ref.refs_8_, ...), custom_call_target="tpu_custom_call" | custom-call | flops 671088640 | bytes 3145728 | tf_op jit(solution)/shard_map/analyse/pallas_call | solution.py:210
  6.6 0.0 copy-start.3
  6.6 0.0 copy-start
  6.6 19.5 %all_to_all.40.in_ref = bf16[8,480,128]{2,1,0:T(8,128)(2,1)S(1)} all-to-all(bf16[8,480,128]{2,1,0:T(8,128)(2,1)S(1)} %analyse.1), channel_id=1, replica_groups=mesh['wide'=32,'narrow'=8] {'narrow'}, dimensions={0} | all-to-all | bytes 1966080 | tf_op jit(solution)/shard_map/all_to_all | solution.py:711
  26.1 0.0 copy-done.1
  26.1 1.0 gather.2
  27.1 10.4 %all-to-all-start.1 = ((bf16[32,2,640]{2,1,0:T(2,128)(2,1)}), bf16[32,2,640]{2,1,0:T(2,128)(2,1)S(1)}, u32[]{:S(2)}, u32[]{:S(2)}) async-start(bf16[32,2,640]{2,1,0:T(2,128)(2,1)} %gather.2), calls=%async_computation.1 | async-start | bytes 163840 | tf_op jit(solution)/shard_map/all_to_all | solution.py:711
  37.5 0.0 copy-done.3
  37.5 0.0 copy-start.4
  37.5 1.1 weight_in.1.weight_ref
  38.6 9.8 %all-to-all-done.1.lines_ref = bf16[32,2,640]{2,1,0:T(2,128)(2,1)S(1)} async-done(((bf16[32,2,640]{2,1,0:T(2,128)(2,1)}), bf16[32,2,640]{2,1,0:T(2,128)(2,1)S(1)}, u32[]{:S(2)}, u32[]{:S(2)}) %all-to-all-start.1) | async-done | bytes 81952 | tf_op jit(solution)/shard_map/all_to_all | solution.py:711
  48.4 0.0 copy-done
  48.4 0.8 mix.1
  49.2 13.9 %all_to_all.41.refs_0_ = bf16[32,2,640]{2,1,0:T(2,128)(2,1)S(1)} all-to-all(bf16[32,2,640]{2,1,0:T(2,128)(2,1)S(1)} %get-tuple-element.19), channel_id=1, replica_groups=mesh['wide'=32,'narrow'=8] {'wide'}, dimensions={0} | all-to-all | bytes 163840 | tf_op jit(solution)/shard_map/all_to_all | solution.py:711
  63.1 1.2 scatter.2
  64.3 5.5 %all-to-all-start.3 = ((bf16[8,320,128]{2,1,0:T(8,128)(2,1)}), bf16[8,320,128]{2,1,0:T(8,128)(2,1)S(1)}, u32[]{:S(2)}, u32[]{:S(2)}) async-start(bf16[8,320,128]{2,1,0:T(8,128)(2,1)} %scatter.2), calls=%async_computation.3 | async-start | bytes 1310720 | tf_op jit(solution)/shard_map/all_to_all | solution.py:711
  69.8 0.0 copy-done.4
  69.8 0.7 broadcast_in_dim.2.refs_5_
  70.5 7.8 %channels.2 = (bf16[20,2,4,32,256]{4,3,2,1,0:T(8,128)(2,1)}, bf16[128,512]{1,0:T(8,128)(2,1)S(1)}, bf16[512,256]{1,0:T(8,128)(2,1)S(1)}, bf16[128,256]{1,0:T(8,128)(2,1)S(1)}, bf16[256,128]{1,0:T(8,128)(2,1)S(1)}) custom-call(s32[1]{0:T(128)} %bitcast.block_ref.refs_0_, bf16[20,2,4,32,256]{4,3,2,1,0:T(8,128)(2,1)} %bitcast.11, bf16[20,20]{1,0:T(8,128)(2,1)} %refs_2_.3, ...), custom_call_target="tpu_custom_call" | custom-call | flops 2000000000 | bytes 6291456 | tf_op jit(solution)/shard_map/channels/pallas_call | solution.py:516
  78.3 1.1 all-to-all-done.3.parts_ref
  79.3 8.6 %local.1 = (bf16[20,2,4,32,256]{4,3,2,1,0:T(8,128)(2,1)}, bf16[20,2,4,32,256]{4,3,2,1,0:T(8,128)(2,1)}, bf16[8,320,128]{2,1,0:T(8,128)(2,1)S(1)}) custom-call(bf16[8,320,128]{2,1,0:T(8,128)(2,1)S(1)} %all-to-all-done.3.parts_ref, bf16[20,2,4,32,256]{4,3,2,1,0:T(8,128)(2,1)} %get-tuple-element.20.mixed_hbm, bf16[20,2,4,32,256]{4,3,2,1,0:T(8,128)(2,1)} %bitcast.9, ...), custom_call_target="tpu_custom_call" | custom-call | flops 1000000000 | bytes 12582912 | tf_op jit(solution)/shard_map/local/pallas_call | solution.py:611
  88.0 14.2 %all_to_all.42.in_ref = bf16[8,320,128]{2,1,0:T(8,128)(2,1)S(1)} all-to-all(bf16[8,320,128]{2,1,0:T(8,128)(2,1)S(1)} %get-tuple-element.26), channel_id=1, replica_groups=mesh['wide'=32,'narrow'=8] {'narrow'}, dimensions={0} | all-to-all | bytes 1310720 | tf_op jit(solution)/shard_map/all_to_all | solution.py:711
  102.2 0.3 gather.3
  102.5 14.1 %all_to_all.43.lines_ref = bf16[32,2,640]{2,1,0:T(2,128)(2,1)S(1)} all-to-all(bf16[32,2,640]{2,1,0:T(2,128)(2,1)S(1)} %gather.3), channel_id=1, replica_groups=mesh['wide'=32,'narrow'=8] {'wide'}, dimensions={0} | all-to-all | bytes 163840 | tf_op jit(solution)/shard_map/all_to_all | solution.py:711
  116.6 0.9 mix_back.1
  117.5 13.9 %all_to_all.44.refs_0_ = bf16[32,2,640]{2,1,0:T(2,128)(2,1)S(1)} all-to-all(bf16[32,2,640]{2,1,0:T(2,128)(2,1)S(1)} %get-tuple-element.28), channel_id=1, replica_groups=mesh['wide'=32,'narrow'=8] {'wide'}, dimensions={0} | all-to-all | bytes 163840 | tf_op jit(solution)/shard_map/all_to_all | solution.py:711
  131.4 1.2 scatter.3
  132.5 4.8 %all-to-all-start.7 = ((bf16[8,336,128]{2,1,0:T(8,128)(2,1)}), bf16[8,336,128]{2,1,0:T(8,128)(2,1)S(1)}, u32[]{:S(2)}, u32[]{:S(2)}) async-start(bf16[8,336,128]{2,1,0:T(8,128)(2,1)} %scatter.3), calls=%async_computation.7 | async-start | bytes 1376256 | tf_op jit(solution)/shard_map/all_to_all | solution.py:711
  137.4 0.0 copy-start.2
  137.4 7.8 %channels.3 = (bf16[20,2,4,32,256]{4,3,2,1,0:T(8,128)(2,1)}, bf16[128,512]{1,0:T(8,128)(2,1)S(1)}) custom-call(s32[1]{0:T(128)} %bitcast.block_ref.refs_0_, bf16[20,2,4,32,256]{4,3,2,1,0:T(8,128)(2,1)} %get-tuple-element.30.refs_1_, bf16[20,20]{1,0:T(8,128)(2,1)} %refs_2_.3, f32[320,20]{1,0:T(8,128)} %constant.31.clone.refs_3_, ...), custom_call_target="tpu_custom_call" | custom-call | flops 2000000000 | bytes 6291456 | tf_op jit(solution)/shard_map/channels/pallas_call | solution.py:516
  145.2 2.1 %all-to-all-done.7.parts_ref = bf16[8,336,128]{2,1,0:T(8,128)(2,1)S(1)} async-done(((bf16[8,336,128]{2,1,0:T(8,128)(2,1)}), bf16[8,336,128]{2,1,0:T(8,128)(2,1)S(1)}, u32[]{:S(2)}, u32[]{:S(2)}) %all-to-all-start.7) | async-done | bytes 688160 | tf_op jit(solution)/shard_map/all_to_all | solution.py:711
  147.3 0.0 copy-done.2
  147.3 4.5 %local_back.1 = (bf16[20,2,4,32,256]{4,3,2,1,0:T(8,128)(2,1)}, f32[2,20,80,32]{3,2,1,0:T(8,128)}) custom-call(bf16[8,336,128]{2,1,0:T(8,128)(2,1)S(1)} %all-to-all-done.7.parts_ref, bf16[20,2,4,32,256]{4,3,2,1,0:T(8,128)(2,1)} %get-tuple-element.31.mixed_hbm, bf16[128,512]{1,0:T(8,128)(2,1)S(1)} %get-tuple-element.32.synth_ref, ...), custom_call_target="tpu_custom_call" | custom-call | flops 2000000000 | bytes 6291456 | tf_op jit(solution)/shard_map/local_back/pallas_call | solution.py:689
Async XLA Ops:
  0.6 25.5 %copy-start.1 = (f32[64,256]{1,0:T(8,128)S(1)}, f32[64,256]{1,0:T(8,128)}, u32[]{:S(2)}) copy-start(f32[64,256]{1,0:T(8,128)} %constant.37.clone.perm_ref.refs_1_) | copy-start | bytes 196612
  6.6 30.9 %copy-start.3 = (f32[128,128]{1,0:T(8,128)S(1)}, f32[128,128]{1,0:T(8,128)}, u32[]{:S(2)}) copy-start(f32[128,128]{1,0:T(8,128)} %constant.36.clone.perm_ref) | copy-start | bytes 196612
  6.6 41.8 %copy-start = (f32[512,256]{1,0:T(8,128)S(1)}, f32[512,256]{1,0:T(8,128)}, u32[]{:S(2)}) copy-start(f32[512,256]{1,0:T(8,128)} %constant.38.clone.first_ref) | copy-start | bytes 1572868
  27.1 21.4 %all-to-all-start.1 = ((bf16[32,2,640]{2,1,0:T(2,128)(2,1)}), bf16[32,2,640]{2,1,0:T(2,128)(2,1)S(1)}, u32[]{:S(2)}, u32[]{:S(2)}) async-start(bf16[32,2,640]{2,1,0:T(2,128)(2,1)} %gather.2), calls=%async_computation.1 | async-start | bytes 163840 | tf_op jit(solution)/shard_map/all_to_all | solution.py:711
  37.5 32.3 %copy-start.4 = (f32[20]{0:T(128)S(1)}, f32[20]{0:T(128)}, u32[]{:S(2)}) copy-start(f32[20]{0:T(128)} %param.21) | copy-start | bytes 244
  64.3 15.0 %all-to-all-start.3 = ((bf16[8,320,128]{2,1,0:T(8,128)(2,1)}), bf16[8,320,128]{2,1,0:T(8,128)(2,1)S(1)}, u32[]{:S(2)}, u32[]{:S(2)}) async-start(bf16[8,320,128]{2,1,0:T(8,128)(2,1)} %scatter.2), calls=%async_computation.3 | async-start | bytes 1310720 | tf_op jit(solution)/shard_map/all_to_all | solution.py:711
  132.5 14.7 %all-to-all-start.7 = ((bf16[8,336,128]{2,1,0:T(8,128)(2,1)}), bf16[8,336,128]{2,1,0:T(8,128)(2,1)S(1)}, u32[]{:S(2)}, u32[]{:S(2)}) async-start(bf16[8,336,128]{2,1,0:T(8,128)(2,1)} %scatter.3), calls=%async_computation.7 | async-start | bytes 1376256 | tf_op jit(solution)/shard_map/all_to_all | solution.py:711
  137.4 9.9 %copy-start.2 = (f32[4,128,32]{2,1,0:T(8,128)S(1)}, f32[4,128,32]{2,1,0:T(8,128)}, u32[]{:S(2)}) copy-start(f32[4,128,32]{2,1,0:T(8,128)} %constant.30.clone.perm_ref) | copy-start | bytes 196612

commit v3 on v2

--- a/solution.py
+++ b/solution.py
@@ -158,12 +158,17 @@
             ].reshape(8, 16, 128)
 
 
+GRID = (C, 2, 4, M, N)
 PARTS = C * 16
 PAIR = PARTS + 16
 STEP = 4
 STEPS = C // STEP
 FIELD_ROWS = STEP * 16
 CARRY_ROWS = FIELD_ROWS + 32
+
+
+VMEM = pl.BlockSpec(memory_space=pltpu.VMEM)
+HBM = pl.BlockSpec(memory_space=pltpu.HBM)
 
 
 def in_hbm(*arrays):
@@ -401,7 +406,32 @@
     )(*operands)
 
 
-def weight_in_kernel(in_ref, perm_ref, out_ref):
+def weight_in_kernel(
+    block_ref,
+    in_ref,
+    perm_ref,
+    synth_ref,
+    depth_ref,
+    table_ref,
+    inverse_ref,
+    back_ref,
+    out_ref,
+    synth_out,
+    depth_out,
+    table_out,
+    inverse_out,
+    back_out,
+):
+    del block_ref
+
+    @pl.when(pl.program_id(0) == 0)
+    def _():
+        synth_out[...] = spread_synth(synth_ref[...])
+        depth_out[...] = spread_depth(depth_ref[...])
+        table_out[...] = table_ref[...].astype(BF)
+        inverse_out[...] = inverse_ref[...].astype(BF)
+        back_out[...] = spread_synth(back_ref[...])
+
     perm = perm_ref[...].astype(BF)
     for b in range(2):
         start = FIELD_ROWS + b * 16
@@ -409,20 +439,30 @@
         out_ref[b * 128 : (b + 1) * 128] = dot_tn(rows, perm)
 
 
-def weight_in(parts, perm):
+def weight_in(block, parts, perm, *tables):
+    shapes = [(128, 512), (2 * N, 256), (128, 256), (256, 128), (128, 512)]
     return pl.pallas_call(
         weight_in_kernel,
-        grid=(STEPS,),
-        in_specs=[
-            pl.BlockSpec((8, CARRY_ROWS, 128), lambda t: (0, t, 0)),
-            pl.BlockSpec((128, 128), lambda t: (0, 0)),
-        ],
-        out_specs=pl.BlockSpec((256, 128), lambda t: (t, 0)),
-        out_shape=jax.ShapeDtypeStruct((STEPS * 256, 128), F32),
-        compiler_params=params(),
-        cost_estimate=cost(2 * 128 * 128 * 1280, MIB),
+        grid_spec=pltpu.PrefetchScalarGridSpec(
+            num_scalar_prefetch=1,
+            grid=(STEPS,),
+            in_specs=[
+                pl.BlockSpec((8, CARRY_ROWS, 128), lambda t, n: (0, t, 0)),
+                whole((128, 128)),
+                whole((2 * M, N)),
+                whole((N, 256)),
+                own((128, 256)),
+                own((256, 128)),
+                whole((2 * M, N)),
+            ],
+            out_specs=[pl.BlockSpec((256, 128), lambda t, n: (t, 0))] + [whole(s) for s in shapes],
+        ),
+        out_shape=[jax.ShapeDtypeStruct((STEPS * 256, 128), F32)]
+        + [jax.ShapeDtypeStruct(s, BF) for s in shapes],
+        compiler_params=params(16),
+        cost_estimate=cost(2 * 128 * 128 * 1280, 3 * MIB),
         name="weight_in",
-    )(parts, perm)
+    )(block, parts, *in_hbm(perm, *tables))
 
 
 def second_inverse(in_ref, table, planes_ref):
@@ -441,94 +481,6 @@
             planes_ref[c + q] = value.astype(BF)
 
 
-GRID_BLOCK = (C, 2, None, 16, N)
-GRID = (C, 2, 4, M, N)
-
-
-def grid_spec():
-    return pl.BlockSpec(GRID_BLOCK, lambda t, *n: (0, 0, t // 2, t % 2, 0))
-
-
-def widen(local_ref, spread_ref, same_ref, transposed):
-    spread = spread_ref[...].astype(BF)
-    multiply = dot_nt if transposed else dot
-    rows = multiply(spread, local_ref[...]).astype(BF)
-    return (dot_nt(rows, spread) * same_ref[...]).astype(BF)
-
-
-def channels_kernel(transposed, *refs):
-    if transposed:
-        _, field_ref, local_ref, spread_ref, same_ref, synth_ref, out_ref, synth_out, wide_ref = refs
-    else:
-        (
-            _,
-            field_ref,
-            local_ref,
-            spread_ref,
-            same_ref,
-            bias_ref,
-            synth_ref,
-            depth_ref,
-            table_ref,
-            inverse_ref,
-            out_ref,
-            synth_out,
-            depth_out,
-            table_out,
-            inverse_out,
-            wide_ref,
-        ) = refs
-
-    @pl.when(pl.program_id(0) == 0)
-    def _():
-        wide_ref[...] = widen(local_ref, spread_ref, same_ref, transposed)
-        synth_out[...] = spread_synth(synth_ref[...])
-        if not transposed:
-            depth_out[...] = spread_depth(depth_ref[...])
-            table_out[...] = table_ref[...].astype(BF)
-            inverse_out[...] = inverse_ref[...].astype(BF)
-
-    for x in range(2):
-        value = dot(wide_ref[...], field_ref[:, x].reshape(C * 16, N)).reshape(C, 16, N)
-        if not transposed:
-            value = value + bias_ref[...]
-        out_ref[:, x] = value.astype(BF)
-
-
-def channels(block, transposed, *operands):
-    grid_shape = pltpu.HBM(GRID, BF)
-    mixing = [whole((C, C)), whole((C * 16, C)), whole((C * 16, C * 16))]
-    synth = whole((2 * M, N))
-    synth_out = whole((128, 512))
-    synth_shape = jax.ShapeDtypeStruct((128, 512), BF)
-    if transposed:
-        in_specs = [grid_spec()] + mixing + [synth]
-        out_specs = [grid_spec(), synth_out]
-        out_shape = [grid_shape, synth_shape]
-    else:
-        in_specs = [grid_spec()] + mixing + [whole((C, 1, N)), synth]
-        in_specs += [whole((N, 256)), own((128, 256)), own((256, 128))]
-        out_specs = [grid_spec(), synth_out]
-        out_specs += [whole((2 * N, 256)), whole((128, 256)), whole((256, 128))]
-        out_shape = [grid_shape, synth_shape] + [
-            jax.ShapeDtypeStruct(s, BF) for s in ((2 * N, 256), (128, 256), (256, 128))
-        ]
-    return pl.pallas_call(
-        functools.partial(channels_kernel, transposed),
-        grid_spec=pltpu.PrefetchScalarGridSpec(
-            num_scalar_prefetch=1,
-            grid=(8,),
-            in_specs=in_specs,
-            out_specs=out_specs,
-            scratch_shapes=[pltpu.VMEM((C * 16, C * 16), BF)],
-        ),
-        out_shape=out_shape,
-        compiler_params=params(16),
-        cost_estimate=cost(2 * 10**9, 6 * MIB),
-        name="channels",
-    )(block, *operands)
-
-
 def piece(ref, t):
     return ref.at[:, :, t // 2, pl.ds(pl.multiple_of((t % 2) * 16, 16), 16), :]
 
@@ -537,60 +489,77 @@
     return pltpu.make_async_copy(piece(source, t), piece(target, t), sem.at[t])
 
 
+def widen(local, transposed):
+    row = lax.broadcasted_iota(jnp.int32, (C * 16, C), 0)
+    channel = lax.broadcasted_iota(jnp.int32, (C * 16, C), 1)
+    spread = jnp.where(row // 16 == channel, 1.0, 0.0).astype(BF)
+    multiply = dot_nt if transposed else dot
+    rows = multiply(spread, local).astype(BF)
+    row = lax.broadcasted_iota(jnp.int32, (C * 16, C * 16), 0)
+    lane = lax.broadcasted_iota(jnp.int32, (C * 16, C * 16), 1)
+    return jnp.where(row % 16 == lane % 16, dot_nt(rows, spread), 0.0).astype(BF)
+
+
 def local_kernel(
     parts_ref,
-    mixed_hbm,
+    field_hbm,
     cotangent_hbm,
     synth_ref,
     depth_ref,
     table_ref,
     inverse_ref,
+    local_ref,
+    bias_ref,
     activated_hbm,
-    slope_hbm,
+    mixed_ref,
     out_ref,
     planes_ref,
     turned_ref,
-    mixed_ref,
+    wide_ref,
+    wide_back_ref,
+    field_ref,
     cotangent_ref,
     activated_ref,
-    slope_ref,
-    mixed_sem,
+    field_sem,
     cotangent_sem,
     activated_sem,
-    slope_sem,
 ):
     for t in range(8):
-        moving(mixed_hbm, mixed_ref, t, mixed_sem).start()
+        moving(field_hbm, field_ref, t, field_sem).start()
         moving(cotangent_hbm, cotangent_ref, t, cotangent_sem).start()
+    wide_ref[...] = widen(local_ref[...], False)
+    wide_back_ref[...] = widen(local_ref[...], True)
     second_inverse(parts_ref, inverse_ref[...], planes_ref)
     scale = 0.7978845608028654
     cubic = scale * 0.044715
 
     def step(t, carry):
-        moving(mixed_hbm, mixed_ref, t, mixed_sem).wait()
+        moving(field_hbm, field_ref, t, field_sem).wait()
         moving(cotangent_hbm, cotangent_ref, t, cotangent_sem).wait()
         y = pl.ds(pl.multiple_of((t % 2) * 16, 16), 16)
         rows = pl.ds(pl.multiple_of(t * 16, 16), 16)
         planes = planes_ref[:, rows, :].reshape(C * 16, 128)
-        spatial = dot(planes, synth_ref[...])
+        left = jnp.concatenate([planes, wide_ref[...]], axis=1)
         slopes = []
         for x in range(2):
+            field = field_ref[:, x, t // 2, y, :].reshape(C * 16, N)
+            right = jnp.concatenate([synth_ref[:, x * N : (x + 1) * N], field], axis=0)
+            values = dot(left, right)
             pieces = []
             for c in range(C):
-                value = spatial[c * 16 : (c + 1) * 16, x * N : (x + 1) * N]
-                value = value + mixed_ref[c, x, t // 2, y, :].astype(F32)
+                value = values[c * 16 : (c + 1) * 16] + bias_ref[c]
                 square = value * value
-                tanh = jnp.tanh(value * (scale + cubic * square))
-                half = 0.5 + 0.5 * tanh
-                activated_ref[c, x, t // 2, y, :] = (value * half).astype(BF)
-                d_inner = (0.5 * scale) + (1.5 * cubic) * square
-                d_gelu = half + value * ((1.0 - tanh * tanh) * d_inner)
-                slope = (cotangent_ref[c, x, t // 2, y, :].astype(F32) * d_gelu).astype(BF)
-                slope_ref[c, x, t // 2, y, :] = slope
-                pieces.append(slope)
-            slopes.append(jnp.concatenate(pieces, axis=0))
+                half = 0.5 + 0.5 * jnp.tanh(value * (scale + cubic * square))
+                activated = value * half
+                activated_ref[c, x, t // 2, y, :] = activated.astype(BF)
+                d_inner = (2.0 * scale) + (6.0 * cubic) * square
+                d_gelu = half + (activated * (1.0 - half)) * d_inner
+                pieces.append((cotangent_ref[c, x, t // 2, y, :].astype(F32) * d_gelu).astype(BF))
+            slope = jnp.concatenate(pieces, axis=0)
+            slopes.append(slope)
+            mixed = dot(wide_back_ref[...], slope).astype(BF)
+            mixed_ref[:, x, t // 2, y, :] = mixed.reshape(C, 16, N)
         moving(activated_ref, activated_hbm, t, activated_sem).start()
-        moving(slope_ref, slope_hbm, t, slope_sem).start()
         response = dot(jnp.concatenate(slopes, axis=1), depth_ref[...])
         turned_ref[:, rows, :] = response.astype(BF).reshape(C, 16, 256)
         return carry
@@ -599,32 +568,31 @@
     second_forward(turned_ref, table_ref[...], out_ref, 0, C)
     for t in range(8):
         moving(activated_ref, activated_hbm, t, activated_sem).wait()
-        moving(slope_ref, slope_hbm, t, slope_sem).wait()
-
-
-VMEM = pl.BlockSpec(memory_space=pltpu.VMEM)
-HBM = pl.BlockSpec(memory_space=pltpu.HBM)
-
-
-def local(parts, mixed, cotangent, *tables):
-    grid_shape = pltpu.HBM(GRID, BF)
+
+
+def local(parts, field, cotangent, *operands):
     return pl.pallas_call(
         local_kernel,
-        in_specs=[VMEM, HBM, HBM] + [VMEM] * len(tables),
-        out_specs=[HBM, HBM, VMEM],
-        out_shape=[grid_shape, grid_shape, jax.ShapeDtypeStruct((8, PARTS, 128), BF)],
+        in_specs=[VMEM, HBM, HBM] + [VMEM] * 5 + [pl.BlockSpec(memory_space=pltpu.SMEM)],
+        out_specs=[HBM, VMEM, VMEM],
+        out_shape=[
+            pltpu.HBM(GRID, BF),
+            jax.ShapeDtypeStruct(GRID, BF),
+            jax.ShapeDtypeStruct((8, PARTS, 128), BF),
+        ],
         scratch_shapes=[pltpu.VMEM((C, 128, 128), BF), pltpu.VMEM((C, 128, 256), BF)]
-        + [pltpu.VMEM(GRID, BF)] * 4
-        + [pltpu.SemaphoreType.DMA((8,))] * 4,
+        + [pltpu.VMEM((C * 16, C * 16), BF)] * 2
+        + [pltpu.VMEM(GRID, BF)] * 3
+        + [pltpu.SemaphoreType.DMA((8,))] * 3,
         compiler_params=params(24),
-        cost_estimate=cost(10**9, 12 * MIB, 1310720),
+        cost_estimate=cost(3 * 10**9, 12 * MIB, 1310720),
         name="local",
-    )(parts, *in_hbm(mixed, cotangent), *tables)
+    )(parts, *in_hbm(field, cotangent), *operands)
 
 
 def local_back_kernel(
     parts_ref,
-    mixed_hbm,
+    mixed_ref,
     synth_ref,
     inverse_ref,
     perm_ref,
@@ -632,16 +600,11 @@
     grad_hbm,
     planes_ref,
     modes_ref,
-    mixed_ref,
     out_ref,
     grad_ref,
-    mixed_sem,
     out_sem,
     grad_sem,
 ):
-    for t in range(8):
-        moving(mixed_hbm, mixed_ref, t, mixed_sem).start()
-
     pair = parts_ref[:, PARTS:, :].reshape(128, 128)
     for i in range(4):
         modes_ref[pl.ds(i, 128, stride=4), :] = dot_tn(pair, perm_ref[i].astype(BF))
@@ -664,7 +627,6 @@
     second_inverse(parts_ref, inverse_ref[...], planes_ref)
 
     def step(t, carry):
-        moving(mixed_hbm, mixed_ref, t, mixed_sem).wait()
         y = pl.ds(pl.multiple_of((t % 2) * 16, 16), 16)
         rows = pl.ds(pl.multiple_of(t * 16, 16), 16)
         planes = planes_ref[:, rows, :].reshape(C * 16, 128)
@@ -688,23 +650,21 @@
     grad = (2, C, 4 * C, M)
     return pl.pallas_call(
         local_back_kernel,
-        in_specs=[VMEM, HBM] + [VMEM] * len(tables),
+        in_specs=[VMEM] * (2 + len(tables)),
         out_specs=[HBM, HBM],
         out_shape=[pltpu.HBM(GRID, BF), pltpu.HBM(grad, F32)],
         scratch_shapes=[
             pltpu.VMEM((C, 128, 128), BF),
             pltpu.VMEM((512, M), F32),
             pltpu.VMEM(GRID, BF),
-            pltpu.VMEM(GRID, BF),
             pltpu.VMEM(grad, F32),
-            pltpu.SemaphoreType.DMA((8,)),
             pltpu.SemaphoreType.DMA((8,)),
             pltpu.SemaphoreType.DMA((4,)),
         ],
         compiler_params=params(24),
         cost_estimate=cost(2 * 10**9, 6 * MIB),
         name="local_back",
-    )(parts, *in_hbm(mixed), *tables)
+    )(parts, mixed, *tables)
 
 
 def exchange(value, axis):
@@ -723,11 +683,6 @@
     perm_line = line_table()
     perm_weight = permutation("Jji", "iJj", sizes)
     perm_modes = permutation("Jji", "jJi", sizes)
-    spread = np.zeros((C * 16, C), np.float32)
-    spread[np.arange(C * 16), np.arange(C * 16) // 16] = 1.0
-    same = bf16(np.equal(np.arange(C * 16)[:, None] % 16, np.arange(C * 16)[None, :] % 16))
-    bias = jnp.broadcast_to(local_bias[:, None, None], (C, 1, N))
-
     perm_grad = np.stack([perm_weight[:, i * M : (i + 1) * M] for i in range(4)])
 
     shape = field.shape
@@ -736,29 +691,30 @@
 
     weight = jnp.transpose(spectral_weight, (0, 1, 2, 3, 5, 4)).reshape(8 * C * C, M)
     parts = exchange(analyse(block, grid_field, weight, forward_b, second, perm_grad), "narrow")
-    mixed, synth, depth, table, table_back = channels(
-        block,
-        False,
-        *in_hbm(grid_field, local_weight, spread, same, bias),
-        *in_hbm(synth_f, inverse_b, second, second_back),
+    weight, synth, depth, table, table_back, back = weight_in(
+        block, parts, perm_modes, synth_f, inverse_b, second, second_back, synth_b
     )
-    weight = weight_in(parts, perm_modes)
     lines = exchange(gather(parts, perm_line, CARRY_ROWS), "wide")
     lines, spectrum = mix(lines, weight, first)
     lines = exchange(lines, "wide")
     parts = exchange(scatter(lines, perm_line), "narrow")
-    activated, slope, parts = local(
-        parts, mixed, grid_cotangent, synth, depth, table, table_back
+    activated, mixed, parts = local(
+        parts,
+        grid_field,
+        grid_cotangent,
+        synth,
+        depth,
+        table,
+        table_back,
+        local_weight,
+        local_bias,
     )
     parts = exchange(parts, "narrow")
-    mixed, synth = channels(
-        block, True, *in_hbm(slope, local_weight, spread, same, synth_b)
-    )
     lines = exchange(gather(parts, perm_line, FIELD_ROWS), "wide")
     lines, pair = mix_back(lines, weight, first, spectrum, perm_modes)
     lines = exchange(lines, "wide")
     parts = exchange(scatter(lines, perm_line, pair), "narrow")
-    field_grad, weight_grad = local_back(parts, mixed, synth, table_back, perm_grad)
+    field_grad, weight_grad = local_back(parts, mixed, back, table_back, perm_grad)
     return (
         activated.reshape(shape),
         field_grad.reshape(shape),

time: 153 us -> 149 us (0.974)
  blocking collectives: 75.5 us -> 103 us
  Pallas kernels: 41.1 us -> 25.8 us
  starting transfers between devices: 20.8 us -> 10.4 us
  waiting for transfers between devices: 13 us -> 8.49 us
    all_to_all x5 -> x7, blocking collectives: 75.5 us -> 103 us  [exchange(): return lax.all_to_all(value, axis, split_axis=0, concat_axis=0, tiled=True)]
    pallas_call x5 -> x3, Pallas kernels: 29.8 us -> 16.2 us  [the longest x1 10.1 us: local(): pl.pallas_call(local_kernel, in_specs=[VMEM, HBM, HBM] + [VMEM] * 5 + [pl...]
    all_to_all x3 -> x1, starting transfers between devices: 20.8 us -> 10.4 us  [exchange(): return lax.all_to_all(value, axis, split_axis=0, concat_axis=0, tiled=True)]
    all_to_all x3 -> x1, waiting for transfers between devices: 13 us -> 8.49 us  [exchange(): return lax.all_to_all(value, axis, split_axis=0, concat_axis=0, tiled=True)]
    pallas_call x2, Pallas kernels: 2.35 us -> 0.66 us  [scatter(): pl.pallas_call(scatter_kernel, out_shape=jax.ShapeDtypeStruct((8, PAIR if...]
  transfers between devices with their start and end apart: 3 -> 1, of which waited for: 3 -> 1; matrix products, arithmetic and copies ran while one was open for 0% -> 0% of each run, Pallas kernels for 11% -> 2%
where the time goes in v3:
time: 149 us; the launch traced here: 148 us
  blocking collectives  103 us (69%)
  Pallas kernels  25.8 us (17%)
  starting transfers between devices  10.4 us (7%)
  waiting for transfers between devices  8.49 us (6%)
    all_to_all x7, blocking collectives, exchange(): return lax.all_to_all(value, axis, split_axis=0, concat_axis=0, tiled=True)  103 us
    all_to_all x1, starting transfers between devices, exchange(): return lax.all_to_all(value, axis, split_axis=0, concat_axis=0, tiled=True)  10.4 us
    pallas_call x1, Pallas kernels, local(): pl.pallas_call(local_kernel, in_specs=[VMEM, HBM, HBM] + [VMEM] * 5 + [pl...  10.1 us
    all_to_all x1, waiting for transfers between devices, exchange(): return lax.all_to_all(value, axis, split_axis=0, concat_axis=0, tiled=True)  8.49 us
    pallas_call x1, Pallas kernels, analyse(): pl.pallas_call(analyse_kernel, grid_spec=pltpu.PrefetchScalarGridSpec(num...  5.93 us
    pallas_call x1, Pallas kernels, local_back(): pl.pallas_call(local_back_kernel, in_specs=[VMEM] * (2 + len(tables)), ou...  3.72 us
  transfers between devices with their start and end apart: 1, of which 1 were waited for; matrix products, arithmetic and copies ran while one was open for 0% of the time, Pallas kernels for 2%

profile of v3, /device:TPU:2, one launch (start us, length us, event | category | flops | bytes accessed | tf_op | source)
XLA Modules:
  0.0 148.5 jit_solution(11916367704658092665)
XLA Ops:
  0.6 0.0 copy-start.1
  0.6 5.9 %analyse.1 = bf16[8,480,128]{2,1,0:T(8,128)(2,1)S(1)} custom-call(s32[1]{0:T(128)} %bitcast.block_ref, bf16[20,2,4,32,256]{4,3,2,1,0:T(8,128)(2,1)} %bitcast.9, f32[3200,32]{1,0:T(8,128)} %bitcast.11, f32[256,256]{1,0:T(8,128)} %constant.24.clone.depth_ref, f32[8,128,256]{2,1,0:T(8,128)} %constant.25.clone.table_ref, f32[4,128,32]{2,1,0:T(8,128)} %constant.26.clone.perm_ref), custom_call_target="tpu_custom_call" | custom-call | flops 671088640 | bytes 3145728 | tf_op jit(solution)/shard_map/analyse/pallas_call | solution.py:215
  6.6 19.4 %all_to_all.40.in_ref = bf16[8,480,128]{2,1,0:T(8,128)(2,1)S(1)} all-to-all(bf16[8,480,128]{2,1,0:T(8,128)(2,1)S(1)} %analyse.1), channel_id=1, replica_groups=mesh['wide'=32,'narrow'=8] {'narrow'}, dimensions={0} | all-to-all | bytes 1966080 | tf_op jit(solution)/shard_map/all_to_all | solution.py:671
  25.9 0.0 copy-done.1
  25.9 0.0 copy-start
  25.9 1.0 gather.2
  26.9 10.4 %all-to-all-start.1 = ((bf16[32,2,640]{2,1,0:T(2,128)(2,1)}), bf16[32,2,640]{2,1,0:T(2,128)(2,1)S(1)}, u32[]{:S(2)}, u32[]{:S(2)}) async-start(bf16[32,2,640]{2,1,0:T(2,128)(2,1)} %gather.2), calls=%async_computation.1 | async-start | bytes 163840 | tf_op jit(solution)/shard_map/all_to_all | solution.py:671
  37.3 2.4 %weight_in.1 = (f32[1280,128]{1,0:T(8,128)S(1)}, bf16[128,512]{1,0:T(8,128)(2,1)S(1)}, bf16[512,256]{1,0:T(8,128)(2,1)S(1)}, bf16[128,256]{1,0:T(8,128)(2,1)S(1)...) custom-call(s32[1]{0:T(128)} %bitcast.block_ref, bf16[8,480,128]{2,1,0:T(8,128)(2,1)S(1)} %all_to_all.40.in_ref, ...), custom_call_target="tpu_custom_call" | custom-call | flops 41943040 | bytes 3145728 | tf_op jit(solution)/shard_map/weight_in/pallas_call | solution.py:444
  39.8 0.0 copy-start.4
  39.8 0.0 copy-start.5
  39.8 8.5 %all-to-all-done.1.lines_ref = bf16[32,2,640]{2,1,0:T(2,128)(2,1)S(1)} async-done(((bf16[32,2,640]{2,1,0:T(2,128)(2,1)}), bf16[32,2,640]{2,1,0:T(2,128)(2,1)S(1)}, u32[]{:S(2)}, u32[]{:S(2)}) %all-to-all-start.1) | async-done | bytes 81952 | tf_op jit(solution)/shard_map/all_to_all | solution.py:671
  48.3 0.0 copy-done
  48.3 0.8 mix.1
  49.1 13.9 %all_to_all.41.refs_0_ = bf16[32,2,640]{2,1,0:T(2,128)(2,1)S(1)} all-to-all(bf16[32,2,640]{2,1,0:T(2,128)(2,1)S(1)} %get-tuple-element.19), channel_id=1, replica_groups=mesh['wide'=32,'narrow'=8] {'wide'}, dimensions={0} | all-to-all | bytes 163840 | tf_op jit(solution)/shard_map/all_to_all | solution.py:671
  63.0 0.3 scatter.2
  63.3 14.1 %all_to_all.42.parts_ref = bf16[8,320,128]{2,1,0:T(8,128)(2,1)S(1)} all-to-all(bf16[8,320,128]{2,1,0:T(8,128)(2,1)S(1)} %scatter.2), channel_id=1, replica_groups=mesh['wide'=32,'narrow'=8] {'narrow'}, dimensions={0} | all-to-all | bytes 1310720 | tf_op jit(solution)/shard_map/all_to_all | solution.py:671
  77.4 0.0 copy-done.4
  77.4 0.0 copy-done.5
  77.4 0.0 copy-start.3
  77.4 10.1 %local.1 = (bf16[20,2,4,32,256]{4,3,2,1,0:T(8,128)(2,1)}, bf16[20,2,4,32,256]{4,3,2,1,0:T(8,128)(2,1)S(1)}, bf16[8,320,128]{2,1,0:T(8,128)(2,1)S(1)}) custom-call(bf16[8,320,128]{2,1,0:T(8,128)(2,1)S(1)} %all_to_all.42.parts_ref, bf16[20,2,4,32,256]{4,3,2,1,0:T(8,128)(2,1)} %bitcast.10, bf16[20,2,4,32,256]{4,3,2,1,0:T(8,128)(2,1)} %bitcast.12, ...), custom_call_target="tpu_custom_call" | custom-call | flops 3000000000 | bytes 12582912 | tf_op jit(solution)/shard_map/local/pallas_call | solution.py:574
  87.5 12.9 %all_to_all.43.in_ref = bf16[8,320,128]{2,1,0:T(8,128)(2,1)S(1)} all-to-all(bf16[8,320,128]{2,1,0:T(8,128)(2,1)S(1)} %get-tuple-element.25), channel_id=1, replica_groups=mesh['wide'=32,'narrow'=8] {'narrow'}, dimensions={0} | all-to-all | bytes 1310720 | tf_op jit(solution)/shard_map/all_to_all | solution.py:671
  100.4 0.0 copy-start.2
  100.4 0.3 gather.3
  100.7 15.2 %all_to_all.44.lines_ref = bf16[32,2,640]{2,1,0:T(2,128)(2,1)S(1)} all-to-all(bf16[32,2,640]{2,1,0:T(2,128)(2,1)S(1)} %gather.3), channel_id=1, replica_groups=mesh['wide'=32,'narrow'=8] {'wide'}, dimensions={0} | all-to-all | bytes 163840 | tf_op jit(solution)/shard_map/all_to_all | solution.py:671
  116.0 0.0 copy-done.3
  116.0 0.9 mix_back.1
  116.8 13.9 %all_to_all.45.refs_0_ = bf16[32,2,640]{2,1,0:T(2,128)(2,1)S(1)} all-to-all(bf16[32,2,640]{2,1,0:T(2,128)(2,1)S(1)} %get-tuple-element.27), channel_id=1, replica_groups=mesh['wide'=32,'narrow'=8] {'wide'}, dimensions={0} | all-to-all | bytes 163840 | tf_op jit(solution)/shard_map/all_to_all | solution.py:671
  130.7 0.3 scatter.3
  131.1 13.7 %all_to_all.46.parts_ref = bf16[8,336,128]{2,1,0:T(8,128)(2,1)S(1)} all-to-all(bf16[8,336,128]{2,1,0:T(8,128)(2,1)S(1)} %scatter.3), channel_id=1, replica_groups=mesh['wide'=32,'narrow'=8] {'narrow'}, dimensions={0} | all-to-all | bytes 1376256 | tf_op jit(solution)/shard_map/all_to_all | solution.py:671
  144.8 0.0 copy-done.2
  144.8 3.7 %local_back.1 = (bf16[20,2,4,32,256]{4,3,2,1,0:T(8,128)(2,1)}, f32[2,20,80,32]{3,2,1,0:T(8,128)}) custom-call(bf16[8,336,128]{2,1,0:T(8,128)(2,1)S(1)} %all_to_all.46.parts_ref, bf16[20,2,4,32,256]{4,3,2,1,0:T(8,128)(2,1)S(1)} %get-tuple-element.29.mixed_ref, bf16[128,512]{1,0:T(8,128)(2,1)S(1)} %get-tuple-element.30.synth_ref, ...), custom_call_target="tpu_custom_call" | custom-call | flops 2000000000 | bytes 6291456 | tf_op jit(solution)/shard_map/local_back/pallas_call | solution.py:651
Async XLA Ops:
  0.6 25.3 %copy-start.1 = (f32[64,256]{1,0:T(8,128)S(1)}, f32[64,256]{1,0:T(8,128)}, u32[]{:S(2)}) copy-start(f32[64,256]{1,0:T(8,128)} %constant.32.clone.perm_ref.refs_1_) | copy-start | bytes 196612
  25.9 22.3 %copy-start = (f32[512,256]{1,0:T(8,128)S(1)}, f32[512,256]{1,0:T(8,128)}, u32[]{:S(2)}) copy-start(f32[512,256]{1,0:T(8,128)} %constant.33.clone.first_ref) | copy-start | bytes 1572868
  26.9 21.4 %all-to-all-start.1 = ((bf16[32,2,640]{2,1,0:T(2,128)(2,1)}), bf16[32,2,640]{2,1,0:T(2,128)(2,1)S(1)}, u32[]{:S(2)}, u32[]{:S(2)}) async-start(bf16[32,2,640]{2,1,0:T(2,128)(2,1)} %gather.2), calls=%async_computation.1 | async-start | bytes 163840 | tf_op jit(solution)/shard_map/all_to_all | solution.py:671
  39.8 37.6 %copy-start.4 = (bf16[20,20]{1,0:T(8,128)(2,1)S(1)}, bf16[20,20]{1,0:T(8,128)(2,1)}, u32[]{:S(2)}) copy-start(bf16[20,20]{1,0:T(8,128)(2,1)} %local_ref.1) | copy-start | bytes 2404
  39.8 37.6 %copy-start.5 = (f32[20]{0:T(128)S(1)}, f32[20]{0:T(128)}, u32[]{:S(2)}) copy-start(f32[20]{0:T(128)} %bias_ref.1) | copy-start | bytes 244
  77.4 38.6 %copy-start.3 = (f32[128,128]{1,0:T(8,128)S(1)}, f32[128,128]{1,0:T(8,128)}, u32[]{:S(2)}) copy-start(f32[128,128]{1,0:T(8,128)} %constant.27.clone.perm_ref) | copy-start | bytes 196612
  100.4 44.4 %copy-start.2 = (f32[4,128,32]{2,1,0:T(8,128)S(1)}, f32[4,128,32]{2,1,0:T(8,128)}, u32[]{:S(2)}) copy-start(f32[4,128,32]{2,1,0:T(8,128)} %constant.26.clone.perm_ref) | copy-start | bytes 196612

commit v4 on v3

--- a/solution.py
+++ b/solution.py
@@ -406,6 +406,17 @@
     )(*operands)
 
 
+def widen(local, transposed):
+    row = lax.broadcasted_iota(jnp.int32, (C * 16, C), 0)
+    channel = lax.broadcasted_iota(jnp.int32, (C * 16, C), 1)
+    spread = jnp.where(row // 16 == channel, 1.0, 0.0).astype(BF)
+    multiply = dot_nt if transposed else dot
+    rows = multiply(spread, local).astype(BF)
+    row = lax.broadcasted_iota(jnp.int32, (C * 16, C * 16), 0)
+    lane = lax.broadcasted_iota(jnp.int32, (C * 16, C * 16), 1)
+    return jnp.where(row % 16 == lane % 16, dot_nt(rows, spread), 0.0).astype(BF)
+
+
 def weight_in_kernel(
     block_ref,
     in_ref,
@@ -415,12 +426,15 @@
     table_ref,
     inverse_ref,
     back_ref,
+    local_ref,
     out_ref,
     synth_out,
     depth_out,
     table_out,
     inverse_out,
     back_out,
+    wide_out,
+    wide_back_out,
 ):
     del block_ref
 
@@ -431,6 +445,8 @@
         table_out[...] = table_ref[...].astype(BF)
         inverse_out[...] = inverse_ref[...].astype(BF)
         back_out[...] = spread_synth(back_ref[...])
+        wide_out[...] = widen(local_ref[...], False)
+        wide_back_out[...] = widen(local_ref[...], True)
 
     perm = perm_ref[...].astype(BF)
     for b in range(2):
@@ -441,6 +457,7 @@
 
 def weight_in(block, parts, perm, *tables):
     shapes = [(128, 512), (2 * N, 256), (128, 256), (256, 128), (128, 512)]
+    shapes += [(C * 16, C * 16)] * 2
     return pl.pallas_call(
         weight_in_kernel,
         grid_spec=pltpu.PrefetchScalarGridSpec(
@@ -454,6 +471,7 @@
                 own((128, 256)),
                 own((256, 128)),
                 whole((2 * M, N)),
+                whole((C, C)),
             ],
             out_specs=[pl.BlockSpec((256, 128), lambda t, n: (t, 0))] + [whole(s) for s in shapes],
         ),
@@ -489,17 +507,6 @@
     return pltpu.make_async_copy(piece(source, t), piece(target, t), sem.at[t])
 
 
-def widen(local, transposed):
-    row = lax.broadcasted_iota(jnp.int32, (C * 16, C), 0)
-    channel = lax.broadcasted_iota(jnp.int32, (C * 16, C), 1)
-    spread = jnp.where(row // 16 == channel, 1.0, 0.0).astype(BF)
-    multiply = dot_nt if transposed else dot
-    rows = multiply(spread, local).astype(BF)
-    row = lax.broadcasted_iota(jnp.int32, (C * 16, C * 16), 0)
-    lane = lax.broadcasted_iota(jnp.int32, (C * 16, C * 16), 1)
-    return jnp.where(row % 16 == lane % 16, dot_nt(rows, spread), 0.0).astype(BF)
-
-
 def local_kernel(
     parts_ref,
     field_hbm,
@@ -508,15 +515,14 @@
     depth_ref,
     table_ref,
     inverse_ref,
-    local_ref,
+    wide_ref,
+    wide_back_ref,
     bias_ref,
     activated_hbm,
     mixed_ref,
     out_ref,
     planes_ref,
     turned_ref,
-    wide_ref,
-    wide_back_ref,
     field_ref,
     cotangent_ref,
     activated_ref,
@@ -527,8 +533,6 @@
     for t in range(8):
         moving(field_hbm, field_ref, t, field_sem).start()
         moving(cotangent_hbm, cotangent_ref, t, cotangent_sem).start()
-    wide_ref[...] = widen(local_ref[...], False)
-    wide_back_ref[...] = widen(local_ref[...], True)
     second_inverse(parts_ref, inverse_ref[...], planes_ref)
     scale = 0.7978845608028654
     cubic = scale * 0.044715
@@ -573,7 +577,7 @@
 def local(parts, field, cotangent, *operands):
     return pl.pallas_call(
         local_kernel,
-        in_specs=[VMEM, HBM, HBM] + [VMEM] * 5 + [pl.BlockSpec(memory_space=pltpu.SMEM)],
+        in_specs=[VMEM, HBM, HBM] + [VMEM] * 6 + [pl.BlockSpec(memory_space=pltpu.SMEM)],
         out_specs=[HBM, VMEM, VMEM],
         out_shape=[
             pltpu.HBM(GRID, BF),
@@ -581,7 +585,6 @@
             jax.ShapeDtypeStruct((8, PARTS, 128), BF),
         ],
         scratch_shapes=[pltpu.VMEM((C, 128, 128), BF), pltpu.VMEM((C, 128, 256), BF)]
-        + [pltpu.VMEM((C * 16, C * 16), BF)] * 2
         + [pltpu.VMEM(GRID, BF)] * 3
         + [pltpu.SemaphoreType.DMA((8,))] * 3,
         compiler_params=params(24),
@@ -639,7 +642,7 @@
         moving(out_ref, out_hbm, t, out_sem).start()
         return carry
 
-    lax.fori_loop(0, 8, step, 0)
+    lax.fori_loop(0, 8, step, 0, unroll=4)
     for t in range(8):
         moving(out_ref, out_hbm, t, out_sem).wait()
     for t in range(4):
@@ -691,8 +694,8 @@
 
     weight = jnp.transpose(spectral_weight, (0, 1, 2, 3, 5, 4)).reshape(8 * C * C, M)
     parts = exchange(analyse(block, grid_field, weight, forward_b, second, perm_grad), "narrow")
-    weight, synth, depth, table, table_back, back = weight_in(
-        block, parts, perm_modes, synth_f, inverse_b, second, second_back, synth_b
+    weight, synth, depth, table, table_back, back, wide, wide_back = weight_in(
+        block, parts, perm_modes, synth_f, inverse_b, second, second_back, synth_b, local_weight
     )
     lines = exchange(gather(parts, perm_line, CARRY_ROWS), "wide")
     lines, spectrum = mix(lines, weight, first)
@@ -706,7 +709,8 @@
         depth,
         table,
         table_back,
-        local_weight,
+        wide,
+        wide_back,
         local_bias,
     )
     parts = exchange(parts, "narrow")

time: 149 us -> 148 us (level)
  no operation moved by 1% of the time
where the time goes in v4:
time: 148 us; the launch traced here: 147 us
  blocking collectives  103 us (70%)
  Pallas kernels  25 us (17%)
  starting transfers between devices  10.4 us (7%)
  waiting for transfers between devices  8 us (5%)
    all_to_all x7, blocking collectives, exchange(): return lax.all_to_all(value, axis, split_axis=0, concat_axis=0, tiled=True)  103 us
    all_to_all x1, starting transfers between devices, exchange(): return lax.all_to_all(value, axis, split_axis=0, concat_axis=0, tiled=True)  10.4 us
    pallas_call x1, Pallas kernels, local(): pl.pallas_call(local_kernel, in_specs=[VMEM, HBM, HBM] + [VMEM] * 6 + [pl...  9.66 us
    all_to_all x1, waiting for transfers between devices, exchange(): return lax.all_to_all(value, axis, split_axis=0, concat_axis=0, tiled=True)  8 us
    pallas_call x1, Pallas kernels, analyse(): pl.pallas_call(analyse_kernel, grid_spec=pltpu.PrefetchScalarGridSpec(num...  5.93 us
  transfers between devices with their start and end apart: 1, of which 1 were waited for; matrix products, arithmetic and copies ran while one was open for 0% of the time, Pallas kernels for 2%

profile of v4, /device:TPU:2, one launch (start us, length us, event | category | flops | bytes accessed | tf_op | source)
XLA Modules:
  0.0 147.2 jit_solution(14258794672770286622)
XLA Ops:
  0.6 0.0 copy-start.1
  0.6 5.9 %analyse.1 = bf16[8,480,128]{2,1,0:T(8,128)(2,1)S(1)} custom-call(s32[1]{0:T(128)} %bitcast.block_ref, bf16[20,2,4,32,256]{4,3,2,1,0:T(8,128)(2,1)} %bitcast.9, f32[3200,32]{1,0:T(8,128)} %bitcast.11, f32[256,256]{1,0:T(8,128)} %constant.24.clone.depth_ref, f32[8,128,256]{2,1,0:T(8,128)} %constant.25.clone.table_ref, f32[4,128,32]{2,1,0:T(8,128)} %constant.26.clone.perm_ref), custom_call_target="tpu_custom_call" | custom-call | flops 671088640 | bytes 3145728 | tf_op jit(solution)/shard_map/analyse/pallas_call | solution.py:215
  6.6 19.4 %all_to_all.40.in_ref = bf16[8,480,128]{2,1,0:T(8,128)(2,1)S(1)} all-to-all(bf16[8,480,128]{2,1,0:T(8,128)(2,1)S(1)} %analyse.1), channel_id=1, replica_groups=mesh['wide'=32,'narrow'=8] {'narrow'}, dimensions={0} | all-to-all | bytes 1966080 | tf_op jit(solution)/shard_map/all_to_all | solution.py:674
  25.9 0.0 copy-done.1
  25.9 0.0 copy-start
  25.9 1.0 gather.2
  26.9 10.4 %all-to-all-start.1 = ((bf16[32,2,640]{2,1,0:T(2,128)(2,1)}), bf16[32,2,640]{2,1,0:T(2,128)(2,1)S(1)}, u32[]{:S(2)}, u32[]{:S(2)}) async-start(bf16[32,2,640]{2,1,0:T(2,128)(2,1)} %gather.2), calls=%async_computation.1 | async-start | bytes 163840 | tf_op jit(solution)/shard_map/all_to_all | solution.py:674
  37.3 2.9 %weight_in.1 = (f32[1280,128]{1,0:T(8,128)S(1)}, bf16[128,512]{1,0:T(8,128)(2,1)S(1)}, bf16[512,256]{1,0:T(8,128)(2,1)S(1)}, bf16[128,256]{1,0:T(8,128)(2,1)S(1)...) custom-call(s32[1]{0:T(128)} %bitcast.block_ref, ...), custom_call_target="tpu_custom_call" | custom-call | flops 41943040 | bytes 3145728 | tf_op jit(solution)/shard_map/weight_in/pallas_call | solution.py:461
  40.3 0.0 copy-start.4
  40.3 8.0 %all-to-all-done.1.lines_ref = bf16[32,2,640]{2,1,0:T(2,128)(2,1)S(1)} async-done(((bf16[32,2,640]{2,1,0:T(2,128)(2,1)}), bf16[32,2,640]{2,1,0:T(2,128)(2,1)S(1)}, u32[]{:S(2)}, u32[]{:S(2)}) %all-to-all-start.1) | async-done | bytes 81952 | tf_op jit(solution)/shard_map/all_to_all | solution.py:674
  48.3 0.0 copy-done
  48.3 0.8 mix.1
  49.1 13.9 %all_to_all.41.refs_0_ = bf16[32,2,640]{2,1,0:T(2,128)(2,1)S(1)} all-to-all(bf16[32,2,640]{2,1,0:T(2,128)(2,1)S(1)} %get-tuple-element.21), channel_id=1, replica_groups=mesh['wide'=32,'narrow'=8] {'wide'}, dimensions={0} | all-to-all | bytes 163840 | tf_op jit(solution)/shard_map/all_to_all | solution.py:674
  63.0 0.3 scatter.2
  63.3 14.1 %all_to_all.42.parts_ref = bf16[8,320,128]{2,1,0:T(8,128)(2,1)S(1)} all-to-all(bf16[8,320,128]{2,1,0:T(8,128)(2,1)S(1)} %scatter.2), channel_id=1, replica_groups=mesh['wide'=32,'narrow'=8] {'narrow'}, dimensions={0} | all-to-all | bytes 1310720 | tf_op jit(solution)/shard_map/all_to_all | solution.py:674
  77.4 0.0 copy-done.4
  77.4 0.0 copy-start.3
  77.4 9.7 %local.1 = (bf16[20,2,4,32,256]{4,3,2,1,0:T(8,128)(2,1)}, bf16[20,2,4,32,256]{4,3,2,1,0:T(8,128)(2,1)S(1)}, bf16[8,320,128]{2,1,0:T(8,128)(2,1)S(1)}) custom-call(bf16[8,320,128]{2,1,0:T(8,128)(2,1)S(1)} %all_to_all.42.parts_ref, bf16[20,2,4,32,256]{4,3,2,1,0:T(8,128)(2,1)} %bitcast.10, bf16[20,2,4,32,256]{4,3,2,1,0:T(8,128)(2,1)} %bitcast.12, ...), custom_call_target="tpu_custom_call" | custom-call | flops 3000000000 | bytes 12582912 | tf_op jit(solution)/shard_map/local/pallas_call | solution.py:578
  87.1 12.9 %all_to_all.43.in_ref = bf16[8,320,128]{2,1,0:T(8,128)(2,1)S(1)} all-to-all(bf16[8,320,128]{2,1,0:T(8,128)(2,1)S(1)} %get-tuple-element.29), channel_id=1, replica_groups=mesh['wide'=32,'narrow'=8] {'narrow'}, dimensions={0} | all-to-all | bytes 1310720 | tf_op jit(solution)/shard_map/all_to_all | solution.py:674
  99.9 0.0 copy-start.2
  99.9 0.3 gather.3
  100.3 15.2 %all_to_all.44.lines_ref = bf16[32,2,640]{2,1,0:T(2,128)(2,1)S(1)} all-to-all(bf16[32,2,640]{2,1,0:T(2,128)(2,1)S(1)} %gather.3), channel_id=1, replica_groups=mesh['wide'=32,'narrow'=8] {'wide'}, dimensions={0} | all-to-all | bytes 163840 | tf_op jit(solution)/shard_map/all_to_all | solution.py:674
  115.5 0.0 copy-done.3
  115.5 0.9 mix_back.1
  116.4 13.9 %all_to_all.45.refs_0_ = bf16[32,2,640]{2,1,0:T(2,128)(2,1)S(1)} all-to-all(bf16[32,2,640]{2,1,0:T(2,128)(2,1)S(1)} %get-tuple-element.31), channel_id=1, replica_groups=mesh['wide'=32,'narrow'=8] {'wide'}, dimensions={0} | all-to-all | bytes 163840 | tf_op jit(solution)/shard_map/all_to_all | solution.py:674
  130.3 0.3 scatter.3
  130.6 13.7 %all_to_all.46.parts_ref = bf16[8,336,128]{2,1,0:T(8,128)(2,1)S(1)} all-to-all(bf16[8,336,128]{2,1,0:T(8,128)(2,1)S(1)} %scatter.3), channel_id=1, replica_groups=mesh['wide'=32,'narrow'=8] {'narrow'}, dimensions={0} | all-to-all | bytes 1376256 | tf_op jit(solution)/shard_map/all_to_all | solution.py:674
  144.3 0.0 copy-done.2
  144.3 2.9 %local_back.1 = (bf16[20,2,4,32,256]{4,3,2,1,0:T(8,128)(2,1)}, f32[2,20,80,32]{3,2,1,0:T(8,128)}) custom-call(bf16[8,336,128]{2,1,0:T(8,128)(2,1)S(1)} %all_to_all.46.parts_ref, bf16[20,2,4,32,256]{4,3,2,1,0:T(8,128)(2,1)S(1)} %get-tuple-element.33.mixed_ref, bf16[128,512]{1,0:T(8,128)(2,1)S(1)} %get-tuple-element.34.synth_ref, ...), custom_call_target="tpu_custom_call" | custom-call | flops 2000000000 | bytes 6291456 | tf_op jit(solution)/shard_map/local_back/pallas_call | solution.py:654
Async XLA Ops:
  0.6 25.3 %copy-start.1 = (f32[64,256]{1,0:T(8,128)S(1)}, f32[64,256]{1,0:T(8,128)}, u32[]{:S(2)}) copy-start(f32[64,256]{1,0:T(8,128)} %constant.32.clone.perm_ref.refs_1_) | copy-start | bytes 196612
  25.9 22.3 %copy-start = (f32[512,256]{1,0:T(8,128)S(1)}, f32[512,256]{1,0:T(8,128)}, u32[]{:S(2)}) copy-start(f32[512,256]{1,0:T(8,128)} %constant.33.clone.first_ref) | copy-start | bytes 1572868
  26.9 21.4 %all-to-all-start.1 = ((bf16[32,2,640]{2,1,0:T(2,128)(2,1)}), bf16[32,2,640]{2,1,0:T(2,128)(2,1)S(1)}, u32[]{:S(2)}, u32[]{:S(2)}) async-start(bf16[32,2,640]{2,1,0:T(2,128)(2,1)} %gather.2), calls=%async_computation.1 | async-start | bytes 163840 | tf_op jit(solution)/shard_map/all_to_all | solution.py:674
  40.3 37.1 %copy-start.4 = (f32[20]{0:T(128)S(1)}, f32[20]{0:T(128)}, u32[]{:S(2)}) copy-start(f32[20]{0:T(128)} %bias_ref.1) | copy-start | bytes 244
  77.4 38.1 %copy-start.3 = (f32[128,128]{1,0:T(8,128)S(1)}, f32[128,128]{1,0:T(8,128)}, u32[]{:S(2)}) copy-start(f32[128,128]{1,0:T(8,128)} %constant.27.clone.perm_ref) | copy-start | bytes 196612
  99.9 44.4 %copy-start.2 = (f32[4,128,32]{2,1,0:T(8,128)S(1)}, f32[4,128,32]{2,1,0:T(8,128)}, u32[]{:S(2)}) copy-start(f32[4,128,32]{2,1,0:T(8,128)} %constant.26.clone.perm_ref) | copy-start | bytes 196612

commit v5 on v4

--- a/solution.py
+++ b/solution.py
@@ -186,6 +186,8 @@
     planes_ref,
     rows_ref,
     depth_scratch,
+    table_scratch,
+    perm_scratch,
 ):
     del block_ref
 
@@ -193,17 +195,19 @@
     def _():
         rows_ref[...] = jnp.zeros((4, 256, M), F32)
         depth_scratch[...] = spread_depth(depth_ref[...])
+        table_scratch[...] = table_ref[...].astype(BF)
+        perm_scratch[...] = perm_ref[...].astype(BF)
 
     rows = jnp.concatenate([field_ref[:, x].reshape(STEP * 128, N) for x in range(2)], axis=1)
     planes_ref[...] = dot(rows, depth_scratch[...]).astype(BF).reshape(STEP, 128, N)
-    second_forward(planes_ref, table_ref[...].astype(BF), out_ref, 0, STEP)
+    second_forward(planes_ref, table_scratch[...], out_ref, 0, STEP)
     got = jnp.zeros((128, 256), F32)
     for i in range(4):
         for q in range(8):
             rows_ref[i, q * CP : q * CP + C, :] = weight_ref[
                 pl.ds(q * 4 * C + i, C, stride=4), :
             ]
-        got = got + dot_nt(perm_ref[i].astype(BF), rows_ref[i].astype(BF))
+        got = got + dot_nt(perm_scratch[i], rows_ref[i].astype(BF))
     got = got.astype(BF)
     for b in range(2):
         out_ref[:, FIELD_ROWS + b * 16 : FIELD_ROWS + (b + 1) * 16, :] = got[
@@ -229,6 +233,8 @@
                 pltpu.VMEM((STEP, 128, 256), BF),
                 pltpu.VMEM((4, 256, M), F32),
                 pltpu.VMEM((2 * N, 256), BF),
+                pltpu.VMEM((128, 256), BF),
+                pltpu.VMEM((4, 128, M), BF),
             ],
         ),
         out_shape=jax.ShapeDtypeStruct((8, STEPS * CARRY_ROWS, 128), BF),

time: 148 us -> 148 us (level)
  no operation moved by 1% of the time
where the time goes in v5:
time: 148 us; the launch traced here: 147 us
  blocking collectives  103 us (70%)
  Pallas kernels  25 us (17%)
  starting transfers between devices  10.4 us (7%)
  waiting for transfers between devices  8 us (5%)
    all_to_all x7, blocking collectives, exchange(): return lax.all_to_all(value, axis, split_axis=0, concat_axis=0, tiled=True)  103 us
    all_to_all x1, starting transfers between devices, exchange(): return lax.all_to_all(value, axis, split_axis=0, concat_axis=0, tiled=True)  10.4 us
    pallas_call x1, Pallas kernels, local(): pl.pallas_call(local_kernel, in_specs=[VMEM, HBM, HBM] + [VMEM] * 6 + [pl...  9.66 us
    all_to_all x1, waiting for transfers between devices, exchange(): return lax.all_to_all(value, axis, split_axis=0, concat_axis=0, tiled=True)  8 us
    pallas_call x1, Pallas kernels, analyse(): pl.pallas_call(analyse_kernel, grid_spec=pltpu.PrefetchScalarGridSpec(num...  5.93 us
  transfers between devices with their start and end apart: 1, of which 1 were waited for; matrix products, arithmetic and copies ran while one was open for 0% of the time, Pallas kernels for 2%

profile of v5, /device:TPU:2, one launch (start us, length us, event | category | flops | bytes accessed | tf_op | source)
XLA Modules:
  0.0 147.2 jit_solution(17905071791377163017)
XLA Ops:
  0.6 0.0 copy-start.1
  0.6 5.9 %analyse.1 = bf16[8,480,128]{2,1,0:T(8,128)(2,1)S(1)} custom-call(s32[1]{0:T(128)} %bitcast.block_ref, bf16[20,2,4,32,256]{4,3,2,1,0:T(8,128)(2,1)} %bitcast.9, f32[3200,32]{1,0:T(8,128)} %bitcast.11, f32[256,256]{1,0:T(8,128)} %constant.24.clone.depth_ref, f32[8,128,256]{2,1,0:T(8,128)} %constant.25.clone.table_ref, f32[4,128,32]{2,1,0:T(8,128)} %constant.26.clone.perm_ref), custom_call_target="tpu_custom_call" | custom-call | flops 671088640 | bytes 3145728 | tf_op jit(solution)/shard_map/analyse/pallas_call | solution.py:219
  6.6 19.4 %all_to_all.40.in_ref = bf16[8,480,128]{2,1,0:T(8,128)(2,1)S(1)} all-to-all(bf16[8,480,128]{2,1,0:T(8,128)(2,1)S(1)} %analyse.1), channel_id=1, replica_groups=mesh['wide'=32,'narrow'=8] {'narrow'}, dimensions={0} | all-to-all | bytes 1966080 | tf_op jit(solution)/shard_map/all_to_all | solution.py:680
  25.9 0.0 copy-done.1
  25.9 0.0 copy-start
  25.9 1.0 gather.2
  26.9 10.4 %all-to-all-start.1 = ((bf16[32,2,640]{2,1,0:T(2,128)(2,1)}), bf16[32,2,640]{2,1,0:T(2,128)(2,1)S(1)}, u32[]{:S(2)}, u32[]{:S(2)}) async-start(bf16[32,2,640]{2,1,0:T(2,128)(2,1)} %gather.2), calls=%async_computation.1 | async-start | bytes 163840 | tf_op jit(solution)/shard_map/all_to_all | solution.py:680
  37.3 2.9 %weight_in.1 = (f32[1280,128]{1,0:T(8,128)S(1)}, bf16[128,512]{1,0:T(8,128)(2,1)S(1)}, bf16[512,256]{1,0:T(8,128)(2,1)S(1)}, bf16[128,256]{1,0:T(8,128)(2,1)S(1)...) custom-call(s32[1]{0:T(128)} %bitcast.block_ref, ...), custom_call_target="tpu_custom_call" | custom-call | flops 41943040 | bytes 3145728 | tf_op jit(solution)/shard_map/weight_in/pallas_call | solution.py:467
  40.3 0.0 copy-start.4
  40.3 8.0 %all-to-all-done.1.lines_ref = bf16[32,2,640]{2,1,0:T(2,128)(2,1)S(1)} async-done(((bf16[32,2,640]{2,1,0:T(2,128)(2,1)}), bf16[32,2,640]{2,1,0:T(2,128)(2,1)S(1)}, u32[]{:S(2)}, u32[]{:S(2)}) %all-to-all-start.1) | async-done | bytes 81952 | tf_op jit(solution)/shard_map/all_to_all | solution.py:680
  48.3 0.0 copy-done
  48.3 0.8 mix.1
  49.1 13.9 %all_to_all.41.refs_0_ = bf16[32,2,640]{2,1,0:T(2,128)(2,1)S(1)} all-to-all(bf16[32,2,640]{2,1,0:T(2,128)(2,1)S(1)} %get-tuple-element.21), channel_id=1, replica_groups=mesh['wide'=32,'narrow'=8] {'wide'}, dimensions={0} | all-to-all | bytes 163840 | tf_op jit(solution)/shard_map/all_to_all | solution.py:680
  63.0 0.3 scatter.2
  63.3 14.1 %all_to_all.42.parts_ref = bf16[8,320,128]{2,1,0:T(8,128)(2,1)S(1)} all-to-all(bf16[8,320,128]{2,1,0:T(8,128)(2,1)S(1)} %scatter.2), channel_id=1, replica_groups=mesh['wide'=32,'narrow'=8] {'narrow'}, dimensions={0} | all-to-all | bytes 1310720 | tf_op jit(solution)/shard_map/all_to_all | solution.py:680
  77.4 0.0 copy-done.4
  77.4 0.0 copy-start.3
  77.4 9.7 %local.1 = (bf16[20,2,4,32,256]{4,3,2,1,0:T(8,128)(2,1)}, bf16[20,2,4,32,256]{4,3,2,1,0:T(8,128)(2,1)S(1)}, bf16[8,320,128]{2,1,0:T(8,128)(2,1)S(1)}) custom-call(bf16[8,320,128]{2,1,0:T(8,128)(2,1)S(1)} %all_to_all.42.parts_ref, bf16[20,2,4,32,256]{4,3,2,1,0:T(8,128)(2,1)} %bitcast.10, bf16[20,2,4,32,256]{4,3,2,1,0:T(8,128)(2,1)} %bitcast.12, ...), custom_call_target="tpu_custom_call" | custom-call | flops 3000000000 | bytes 12582912 | tf_op jit(solution)/shard_map/local/pallas_call | solution.py:584
  87.1 12.9 %all_to_all.43.in_ref = bf16[8,320,128]{2,1,0:T(8,128)(2,1)S(1)} all-to-all(bf16[8,320,128]{2,1,0:T(8,128)(2,1)S(1)} %get-tuple-element.29), channel_id=1, replica_groups=mesh['wide'=32,'narrow'=8] {'narrow'}, dimensions={0} | all-to-all | bytes 1310720 | tf_op jit(solution)/shard_map/all_to_all | solution.py:680
  99.9 0.0 copy-start.2
  99.9 0.3 gather.3
  100.3 15.2 %all_to_all.44.lines_ref = bf16[32,2,640]{2,1,0:T(2,128)(2,1)S(1)} all-to-all(bf16[32,2,640]{2,1,0:T(2,128)(2,1)S(1)} %gather.3), channel_id=1, replica_groups=mesh['wide'=32,'narrow'=8] {'wide'}, dimensions={0} | all-to-all | bytes 163840 | tf_op jit(solution)/shard_map/all_to_all | solution.py:680
  115.5 0.0 copy-done.3
  115.5 0.9 mix_back.1
  116.4 13.9 %all_to_all.45.refs_0_ = bf16[32,2,640]{2,1,0:T(2,128)(2,1)S(1)} all-to-all(bf16[32,2,640]{2,1,0:T(2,128)(2,1)S(1)} %get-tuple-element.31), channel_id=1, replica_groups=mesh['wide'=32,'narrow'=8] {'wide'}, dimensions={0} | all-to-all | bytes 163840 | tf_op jit(solution)/shard_map/all_to_all | solution.py:680
  130.3 0.3 scatter.3
  130.6 13.7 %all_to_all.46.parts_ref = bf16[8,336,128]{2,1,0:T(8,128)(2,1)S(1)} all-to-all(bf16[8,336,128]{2,1,0:T(8,128)(2,1)S(1)} %scatter.3), channel_id=1, replica_groups=mesh['wide'=32,'narrow'=8] {'narrow'}, dimensions={0} | all-to-all | bytes 1376256 | tf_op jit(solution)/shard_map/all_to_all | solution.py:680
  144.3 0.0 copy-done.2
  144.3 2.9 %local_back.1 = (bf16[20,2,4,32,256]{4,3,2,1,0:T(8,128)(2,1)}, f32[2,20,80,32]{3,2,1,0:T(8,128)}) custom-call(bf16[8,336,128]{2,1,0:T(8,128)(2,1)S(1)} %all_to_all.46.parts_ref, bf16[20,2,4,32,256]{4,3,2,1,0:T(8,128)(2,1)S(1)} %get-tuple-element.33.mixed_ref, bf16[128,512]{1,0:T(8,128)(2,1)S(1)} %get-tuple-element.34.synth_ref, ...), custom_call_target="tpu_custom_call" | custom-call | flops 2000000000 | bytes 6291456 | tf_op jit(solution)/shard_map/local_back/pallas_call | solution.py:660
Async XLA Ops:
  0.6 25.3 %copy-start.1 = (f32[64,256]{1,0:T(8,128)S(1)}, f32[64,256]{1,0:T(8,128)}, u32[]{:S(2)}) copy-start(f32[64,256]{1,0:T(8,128)} %constant.32.clone.perm_ref.refs_1_) | copy-start | bytes 196612
  25.9 22.3 %copy-start = (f32[512,256]{1,0:T(8,128)S(1)}, f32[512,256]{1,0:T(8,128)}, u32[]{:S(2)}) copy-start(f32[512,256]{1,0:T(8,128)} %constant.33.clone.first_ref) | copy-start | bytes 1572868
  26.9 21.4 %all-to-all-start.1 = ((bf16[32,2,640]{2,1,0:T(2,128)(2,1)}), bf16[32,2,640]{2,1,0:T(2,128)(2,1)S(1)}, u32[]{:S(2)}, u32[]{:S(2)}) async-start(bf16[32,2,640]{2,1,0:T(2,128)(2,1)} %gather.2), calls=%async_computation.1 | async-start | bytes 163840 | tf_op jit(solution)/shard_map/all_to_all | solution.py:680
  40.3 37.1 %copy-start.4 = (f32[20]{0:T(128)S(1)}, f32[20]{0:T(128)}, u32[]{:S(2)}) copy-start(f32[20]{0:T(128)} %bias_ref.1) | copy-start | bytes 244
  77.4 38.1 %copy-start.3 = (f32[128,128]{1,0:T(8,128)S(1)}, f32[128,128]{1,0:T(8,128)}, u32[]{:S(2)}) copy-start(f32[128,128]{1,0:T(8,128)} %constant.27.clone.perm_ref) | copy-start | bytes 196612
  99.9 44.4 %copy-start.2 = (f32[4,128,32]{2,1,0:T(8,128)S(1)}, f32[4,128,32]{2,1,0:T(8,128)}, u32[]{:S(2)}) copy-start(f32[4,128,32]{2,1,0:T(8,128)} %constant.26.clone.perm_ref) | copy-start | bytes 196612
